TPU v7x, 128 devices: a whole 4x4x4 slice. The times are simulated.
128 devices in a mesh: dp: 2 (over x_lo), seq: 16 (over x_hi, z, core), mp: 4 (over y).
Axes of the slice: x: 4 (x_hi: 2, x_lo: 2; x = x_hi * 2 + x_lo), y: 4, z: 4, core: 2. Of those that a mesh axis runs over, the one named last changes fastest.
Arguments:
- enc_out: bfloat16 [2, 4096, 4096], P('dp', 'seq'), may hold values from -6 to 6
- dec_query: bfloat16 [2, 4096, 2048], P('dp', 'seq', 'mp'), may hold values from -64 to 64
- ctx_grad: bfloat16 [2, 4096, 2048], P('dp', 'seq', 'mp'), may hold values from -6 to 6
- kv_weight: bfloat16 [2, 4096, 2048], P(None, ('dp', 'seq'), 'mp'), may hold values from -0.09375 to 0.09375
- enc_seg: int32 [2, 4096], P('dp'), may hold values from 0 to 3, never falling along the last dimension, each value on 1 to 2048 neighbouring positions
- dec_seg: int32 [2, 4096], P('dp', 'seq'), may hold values from 0 to 3, never falling along the last dimension, each value on 1 to 2048 neighbouring positions
Outputs:
- enc_grad: bfloat16 [2, 4096, 4096], P('dp', 'seq', 'mp')
- query_grad: bfloat16 [2, 4096, 2048], P('dp', 'seq', 'mp')
- kv_weight_grad: float32 [2, 4096, 2048], P(None, ('dp', 'seq'), 'mp')
Inputs may be any that keep to these rules, and one draw needn't show every extreme that they name: `enc_seg`: each replica's ids never fall along the positions, every id appears, and each pair covers at most 2048 positions. `dec_seg`: each replica's ids never fall along the positions, every id appears, and each pair covers at most 2048 positions.
All inputs are finite; a program needn't handle non-finite values.
Results may differ from a plain program's by a relative error of at most 0.034.
The roundings to bfloat16 on the way count: a program that leaves them out, or rounds other values in their place, can miss the bound.
Values may be sent and summed in bfloat16 or wider, within the bound.
A program may use at most 128 MiB of HBM per device.

v0:
```python
import jax
import jax.numpy as jnp
from jax import lax
from jax.sharding import PartitionSpec as P

DH = 64


SCALE = 0.125
NEG = -1e30


def head_backward(query, grad_out, keys, values, mask):
    scores = jnp.where(
        mask, jnp.dot(query, keys.T, preferred_element_type=jnp.float32) * SCALE, NEG
    )
    top = jnp.max(scores, axis=-1, keepdims=True)
    weights = jnp.exp(scores - top)
    probs = weights / jnp.sum(weights, axis=-1, keepdims=True)
    probs_low = probs.astype(jnp.bfloat16)
    context = jnp.dot(probs_low, values, preferred_element_type=jnp.float32)
    delta = jnp.sum(grad_out.astype(jnp.float32) * context, axis=-1, keepdims=True)
    dprobs = jnp.dot(grad_out, values.T, preferred_element_type=jnp.float32)
    dscores = (probs * (dprobs - delta) * SCALE).astype(jnp.bfloat16)
    return (probs_low, dscores, jnp.dot(dscores, keys, preferred_element_type=jnp.float32))


def body(enc_out, dec_query, ctx_grad, kv_weight, enc_seg, dec_seg):
    full_weight = lax.all_gather(kv_weight, ("dp", "seq"), axis=1, tiled=True)
    encoder = enc_out[0]
    width = kv_weight.shape[2]
    head_count = width // DH
    projected = jnp.einsum(
        "td,cdh->cth", encoder, full_weight, preferred_element_type=jnp.float32
    ).astype(jnp.bfloat16)
    all_keys = lax.all_gather(projected, "seq", axis=1, tiled=True)
    mask = dec_seg[0][:, None] == enc_seg[0][None, :]

    def split_heads(array):
        return array.reshape(array.shape[0], head_count, DH).transpose(1, 0, 2)

    def join_heads(array):
        return array.transpose(1, 0, 2).reshape(array.shape[1], head_count * DH)

    def one_head(items):
        query, grad_out, keys, values = items
        probs_low, dscores, dquery = head_backward(query, grad_out, keys, values, mask)
        dkeys = jnp.dot(dscores.T, query, preferred_element_type=jnp.float32)
        dvalues = jnp.dot(probs_low.T, grad_out, preferred_element_type=jnp.float32)
        return (dquery, dkeys, dvalues)

    dquery, dkeys, dvalues = lax.map(
        one_head,
        (
            split_heads(dec_query[0]),
            split_heads(ctx_grad[0]),
            split_heads(all_keys[0]),
            split_heads(all_keys[1]),
        ),
    )
    query_out = join_heads(dquery).astype(jnp.bfloat16)[None]
    key_terms = jnp.stack(
        [join_heads(dkeys).astype(jnp.bfloat16), join_heads(dvalues).astype(jnp.bfloat16)]
    )
    kv_grads = (
        lax.psum_scatter(key_terms, "seq", scatter_dimension=1, tiled=True)
        .astype(jnp.float32)
        .astype(jnp.bfloat16)
    )
    enc_term = jnp.einsum("cth,cdh->td", kv_grads, full_weight, preferred_element_type=jnp.float32)
    enc_grad = lax.psum_scatter(
        enc_term.astype(jnp.bfloat16), "mp", scatter_dimension=1, tiled=True
    )[None]
    row_count = kv_weight.shape[1]
    term = jnp.einsum("tr,cth->rch", encoder, kv_grads, preferred_element_type=jnp.float32)
    summed = lax.psum_scatter(
        term.reshape(lax.axis_size(("dp", "seq")) * row_count, 2 * width).astype(jnp.bfloat16),
        ("dp", "seq"),
        scatter_dimension=0,
        tiled=True,
    ).astype(jnp.float32)
    weight_grad = summed.reshape(row_count, 2, width).transpose(1, 0, 2)
    return (enc_grad, query_out, weight_grad)


def solution(mesh):
    placed = (
        P("dp", "seq", None),
        P("dp", "seq", "mp"),
        P("dp", "seq", "mp"),
        P(None, ("dp", "seq"), "mp"),
        P("dp", None),
        P("dp", "seq"),
    )
    return jax.shard_map(
        body,
        mesh=mesh,
        in_specs=placed,
        out_specs=(P("dp", "seq", "mp"), P("dp", "seq", "mp"), P(None, ("dp", "seq"), "mp")),
        check_vma=False,
    )
```

profile of v0, /device:TPU:1, one launch (start us, length us, event | category | flops | bytes accessed | tf_op | source)
XLA Modules:
  0.0 621.8 jit_solution(10711557607021571431)
XLA Ops:
  9.3 89.5 %all-gather.3.cloned.1.call-done = bf16[2,4096,512]{1,2,0:T(8,128)(2,1)} async-done(((bf16[2,128,512]{1,2,0:T(8,128)(2,1)}), bf16[2,4096,512]{1,2,0:T(8,128)(2,1)}) %all-gather.3.cloned.1.call-update) | async-done | bytes 8388624 | tf_op jit(solution)/shard_map/all_gather | solution.py:29
  98.8 6.5 %fusion.45 = bf16[2,256,512]{1,2,0:T(8,128)(2,1)} fusion(bf16[2,4096,512]{1,2,0:T(8,128)(2,1)} %all-gather.3.cloned.1.call-done, bf16[1,256,4096]{2,1,0:T(8,128)(2,1)S(1)} %copy-done), kind=kOutput, calls=%fused_computation.50 | convolution fusion | flops 2147745792 | bytes 11010048 | tf_op jit(solution)/shard_map/td,cdh->cth/dot_general | solution.py:33
  105.8 76.2 %all-gather.5.cloned.1.call-done = bf16[2,4096,512]{1,2,0:T(8,128)(2,1)} async-done(((bf16[2,256,512]{1,2,0:T(8,128)(2,1)}), bf16[2,4096,512]{1,2,0:T(8,128)(2,1)}) %all-gather.5.cloned.1.call-update) | async-done | bytes 8388624 | tf_op jit(solution)/shard_map/all_gather | solution.py:36
  182.0 6.1 fusion.49
  188.1 8.4 %copy.30 = bf16[4096,8,64]{2,0,1:T(8,128)(2,1)} copy(bf16[4096,8,64]{0,2,1:T(8,128)(2,1)} %bitcast.122) | data formatting | bytes 8388608 | tf_op jit(solution)/shard_map/reshape;squeeze | solution.py:40
  196.5 8.4 %copy.28 = bf16[4096,8,64]{2,0,1:T(8,128)(2,1)} copy(bf16[4096,8,64]{0,2,1:T(8,128)(2,1)} %bitcast.121) | data formatting | bytes 8388608 | tf_op jit(solution)/shard_map/reshape;squeeze | solution.py:40
  204.9 106.1 %while.15 = (s32[]{:T(128)}, bf16[8,256,64]{1,2,0:T(8,128)(2,1)S(1)}, bf16[8,4096,64]{1,2,0:T(8,128)(2,1)}, bf16[8,4096,64]{1,2,0:T(8,128)(2,1)}, bf16[8,256,64]...) while((s32[]{:T(128)}, ...), condition=%wide.region_4.5_spmd.clone, body=%wide.region_0.4_spmd.clone.sunk | while | flops 824229120 | bytes 33818732 | solution.py:52
  204.9 2.4 fusion.83
  212.1 2.8 fusion.86
  218.2 2.4 fusion.83
  225.4 2.8 fusion.86
  231.5 2.4 fusion.83
  236.4 2.3 fusion.85
  238.6 2.8 fusion.86
  244.7 2.4 fusion.83
  249.6 2.3 fusion.85
  251.9 2.8 fusion.86
  258.0 2.4 fusion.83
  265.1 2.8 fusion.86
  271.3 2.4 fusion.83
  278.4 2.8 fusion.86
  284.5 2.4 fusion.83
  291.7 2.8 fusion.86
  297.7 2.4 fusion.83
  304.9 2.8 fusion.86
  311.0 7.5 %pad_maximum_fusion = bf16[2,4096,512]{1,2,0:T(8,128)(2,1)} fusion(bf16[1,4096,512]{1,2,0:T(8,128)(2,1)} %bitcast.124, bf16[1,4096,512]{1,2,0:T(8,128)(2,1)} %bitcast.14), kind=kLoop, calls=%fused_computation.42 | loop fusion | flops 4194304 | bytes 16777216 | tf_op jit(solution)/shard_map/stack | solution.py:62
  318.7 98.4 %reduce-scatter.6.cloned.1.call-done = bf16[2,256,512]{1,2,0:T(8,128)(2,1)} async-done(((bf16[2,4096,512]{1,2,0:T(8,128)(2,1)}), bf16[2,256,512]{1,2,0:T(8,128)(2,1)}) %reduce-scatter.6.cloned.1.call-update) | async-done | bytes 524304 | tf_op jit(solution)/shard_map/reduce_scatter | solution.py:66
  417.1 6.6 %convolution_convert_fusion = bf16[2,512,4096]{2,1,0:T(8,128)(2,1)} fusion(bf16[2,256,512]{1,2,0:T(8,128)(2,1)} %reduce-scatter.6.cloned.1.call-done, bf16[1,256,4096]{2,1,0:T(8,128)(2,1)S(1)} %copy-done), kind=kOutput, calls=%fused_computation.43 | convolution fusion | flops 2151677952 | bytes 11010048 | tf_op jit(solution)/shard_map/tr,cth->rch/dot_general | solution.py:75
  423.8 12.0 %copy.38 = bf16[4096,1024]{1,0:T(8,128)(2,1)} copy(bf16[4096,1024]{0,1:T(8,128)(2,1)} %bitcast.119) | data formatting | bytes 16777216
  436.8 7.1 %fusion.38 = bf16[256,4096]{1,0:T(8,128)(2,1)} fusion(bf16[2,256,512]{1,2,0:T(8,128)(2,1)S(1)} %copy-done.1, bf16[2,4096,512]{1,2,0:T(8,128)(2,1)} %all-gather.3.cloned.1.call-done), kind=kOutput, calls=%fused_computation.45 | convolution fusion | flops 2148532224 | bytes 11010048 | tf_op jit(solution)/shard_map/cth,cdh->td/dot_general | solution.py:70
  444.7 131.3 %reduce-scatter.10.cloned.1.call-done = bf16[128,1024]{1,0:T(8,128)(2,1)} async-done(((bf16[4096,1024]{1,0:T(8,128)(2,1)}), bf16[128,1024]{1,0:T(8,128)(2,1)}) %reduce-scatter.10.cloned.1.call-update) | async-done | bytes 262160
  578.2 37.0 %reduce-scatter.8.cloned.1.call-done = bf16[256,1024]{1,0:T(8,128)(2,1)} async-done(((bf16[256,4096]{1,0:T(8,128)(2,1)}), bf16[256,1024]{1,0:T(8,128)(2,1)}) %reduce-scatter.8.cloned.1.call-update) | async-done | bytes 524304 | tf_op jit(solution)/shard_map/reduce_scatter | solution.py:71
  (70 shorter events, 66.5 us)
Async XLA Ops:
  7.2 91.6 %copy-start = (bf16[1,256,4096]{2,1,0:T(8,128)(2,1)S(1)}, bf16[1,256,4096]{2,1,0:T(8,128)(2,1)}, u32[]{:S(2)}) copy-start(bf16[1,256,4096]{2,1,0:T(8,128)(2,1)} %param.8) | copy-start | bytes 6291460
  7.2 91.6 %all-gather.3.cloned.1.call-start = ((), (), s32[]{:S(2)}) async-start(), calls=%async_computation.3 | async-start | bytes 8650752 | tf_op jit(solution)/shard_map/all_gather | solution.py:29
  9.2 96.3 %copy-start.2 = (bf16[1,256,512]{2,1,0:T(8,128)(2,1)S(1)}, bf16[1,256,512]{2,1,0:T(8,128)(2,1)}, u32[]{:S(2)}) copy-start(bf16[1,256,512]{2,1,0:T(8,128)(2,1)} %param.9) | copy-start | bytes 786436
  9.2 96.4 %copy-start.3 = (bf16[1,256,512]{2,1,0:T(8,128)(2,1)S(1)}, bf16[1,256,512]{2,1,0:T(8,128)(2,1)}, u32[]{:S(2)}) copy-start(bf16[1,256,512]{2,1,0:T(8,128)(2,1)} %param.10) | copy-start | bytes 786436
  9.2 172.8 %all-gather.5.cloned.1.call-start = ((), (), s32[]{:S(2)}) async-start(), calls=%async_computation.4 | async-start | bytes 8912896 | tf_op jit(solution)/shard_map/all_gather | solution.py:36
  105.4 311.8 %reduce-scatter.6.cloned.1.call-start = ((), (), s32[]{:S(2)}) async-start(), calls=%async_computation.5 | async-start | bytes 8912896 | tf_op jit(solution)/shard_map/reduce_scatter | solution.py:66
  196.5 8.4 %copy-start.4 = (s32[1,4096]{1,0:T(1,128)S(1)}, s32[1,4096]{1,0:T(1,128)}, u32[]{:S(2)}) copy-start(s32[1,4096]{1,0:T(1,128)} %param.12) | copy-start | bytes 49156
  196.5 8.4 %copy-start.5 = (s32[1,256]{1,0:T(1,128)S(1)}, s32[1,256]{1,0:T(1,128)}, u32[]{:S(2)}) copy-start(s32[1,256]{1,0:T(1,128)} %param.13) | copy-start | bytes 3076
  318.5 257.6 %reduce-scatter.10.cloned.1.call-start = ((), (), s32[]{:S(2)}) async-start(), calls=%async_computation.7 | async-start | bytes 8650752
  435.7 1.0 copy-start.1
  435.8 179.5 %reduce-scatter.8.cloned.1.call-start = ((), (), s32[]{:S(2)}) async-start(), calls=%async_computation.6 | async-start | bytes 2621440 | tf_op jit(solution)/shard_map/reduce_scatter | solution.py:71
Sparse Core Ops, SparseCore 0:
  10.2 88.5 all-gather.2
  105.5 76.4 all-gather.4
  318.6 98.4 reduce-scatter.5
  435.9 140.1 reduce-scatter.9
  578.9 36.3 reduce-scatter.7
where the time goes:
time: 624 us; the launch traced here: 622 us
  waiting for transfers between devices  433 us (69%)
  matrix products  120 us (19%)
  local copies, waits for them, and re-layouts  41.1 us (7%)
  between operations  13.9 us (2%)
  other arithmetic  13.2 us (2%)
    unnamed x6, waiting for transfers between devices  131 us
    reduce_scatter x1, waiting for transfers between devices, body(): lax.psum_scatter(key_terms, 'seq', scatter_dimension=1, tiled=True)  98.4 us
    all_gather x1, waiting for transfers between devices, body(): full_weight = lax.all_gather(kv_weight, ('dp', 'seq'), axis=1, tiled=True)  89.5 us
    all_gather x1, waiting for transfers between devices, body(): all_keys = lax.all_gather(projected, 'seq', axis=1, tiled=True)  76.2 us
    reduce_scatter x1, waiting for transfers between devices, body(): lax.psum_scatter(enc_term.astype(jnp.bfloat16), 'mp', scatter_dimension=1...  37 us
    dot_general x8, matrix products, head_backward(): dprobs = jnp.dot(grad_out, values.T, preferred_element_type=jnp.float32)  22.3 us
    dot_general x8, matrix products, head_backward(): jnp.dot(query, keys.T, preferred_element_type=jnp.float32) * SCALE  19.1 us
    dot_general x8, matrix products, head_backward(): context = jnp.dot(probs_low, values, preferred_element_type=jnp.float32)  18.1 us
  transfers between devices with their start and end apart: 5, of which 5 were waited for; matrix products, arithmetic and copies ran while one was open for 2% of the time, Pallas kernels for 0%

commit v1 on v0

v1 whole, which is shorter than its diff:
```python
import functools

import jax
import jax.numpy as jnp
from jax import lax
from jax.experimental import pallas as pl
from jax.experimental.pallas import tpu as pltpu
from jax.sharding import PartitionSpec as P

MESH = pl.DeviceIdType.MESH
BF = jnp.bfloat16
F32 = jnp.float32
NEG = -1e30
KB = 256
RING = (2, 1, 3)


def coords():
    dp, seq, y = lax.axis_index("dp"), lax.axis_index("seq"), lax.axis_index("mp")
    xh = seq // 8
    return xh * 2 + dp, xh, (seq // 2) % 4, seq % 2, y


def dev(x, z, core, y):
    return (x % 2, (x // 2) * 8 + z * 2 + core, y)


def row_group(x):
    return (x % 2) * 2 + x // 2


def mod4(v):
    return (v + 4) % 4


def remote(src, dst, send, recv, device):
    return pltpu.make_async_remote_copy(
        src_ref=src, dst_ref=dst, send_sem=send, recv_sem=recv, device_id=device, device_id_type=MESH
    )


def arrived(dst, sem):
    pltpu.make_async_copy(dst, dst, sem).wait()


def greet(peers):
    barrier = pltpu.get_barrier_semaphore()
    for peer in peers:
        pl.semaphore_signal(barrier, inc=1, device_id=peer, device_id_type=MESH)
    pl.semaphore_wait(barrier, len(peers))


def lanes_of(shape):
    return lax.broadcasted_iota(jnp.int32, shape, 1)


def halves(first, second, shift_first, shift_second):
    first = pltpu.roll(first, 64, 1) if shift_first else first
    second = pltpu.roll(second, 64, 1) if shift_second else second
    return jnp.where(lanes_of(first.shape) < 64, first, second)


def front(
    enc, q, do, w, dseg, eseg,
    wg_out, kvx, kvt, xt, xs, dec_out,
    encv, wg, acc, kvs, kvb, qs, qb,
    loc, sib_s, sib_r, ws, wr, qsend, qrecv, ksend, krecv,
):
    x, xh, z, c, y = coords()
    me = row_group(x)
    t = xh * 4 + z
    sibling = dev(x, z, 1 - c, y)
    peers = [sibling]
    for dx in range(4):
        for dz in range(4):
            if dx == 0 and dz == 0:
                continue
            if dx in (0, 2) or dz == 0:
                peers.append(dev(mod4(x + dx), mod4(z + dz), c, y))
            if dx in (0, 2):
                peers.append(dev(mod4(x + dx), mod4(z + dz), 1 - c, y))
    greet(peers)

    own = pl.multiple_of(c * 256, 256)
    other = pl.multiple_of((1 - c) * 256, 256)
    rows = pl.ds(pl.multiple_of(c * 128, 128), 128)
    w_sib = remote(w.at[:, :, pl.ds(other, 256)], wg.at[:, me, z, rows], sib_s.at[0], sib_r.at[0], sibling)
    w_sib.start()
    w_loc = pltpu.make_async_copy(w.at[:, :, pl.ds(own, 256)], wg.at[:, me, z, rows], loc.at[0])
    w_loc.start()
    e_sib = remote(enc, encv.at[c], sib_s.at[1], sib_r.at[1], sibling)
    e_sib.start()
    e_loc = pltpu.make_async_copy(enc, encv.at[c], loc.at[1])
    e_loc.start()
    w_loc.wait()
    w_sib.wait()

    def to(a, dx, dz, step_x, step_z):
        bx, bz = mod4(x - (dx - step_x)), mod4(z - (dz - step_z))
        block = wg.at[a, row_group(bx), bz]
        copy = remote(
            block, block, ws.at[a, dx, dz], wr.at[a, dx, dz], dev(mod4(x + step_x), mod4(z + step_z), c, y)
        )
        copy.start()
        return copy

    sent = []
    for d in RING:
        sent.append(to(0, d, 0, d, 0))
        sent.append(to(1, 0, d, 0, d))
    for d in RING:
        sent.append(to(0, 0, d, 0, d))
        sent.append(to(1, d, 0, d, 0))

    for h in range(8):
        tile = pl.ds((h // 2) * 128, 128)
        odd = h % 2 == 1
        qs[h, 0:256, :] = halves(q[:, tile].astype(F32), do[:, tile].astype(F32), odd, not odd).astype(BF)
        qs[h, 256:272, :] = dseg[...].astype(BF)
    q_sent = []
    for dxh in (1, 0):
        for dz in (2, 1, 3, 0):
            if dxh == 0 and dz == 0:
                continue
            hx, hz = (xh + dxh) % 2, mod4(z + dz)
            copy = remote(
                qs.at[hx * 4 + hz], qb.at[t], qsend.at[dxh, dz], qrecv.at[dxh, dz],
                dev(mod4(x + 2 * dxh), hz, c, y),
            )
            copy.start()
            q_sent.append(copy)
    q_loc = pltpu.make_async_copy(qs.at[t], qb.at[t], loc.at[2])
    q_loc.start()

    def block_at(a, dx, dz):
        return wg.at[a, row_group(mod4(x - dx)), mod4(z - dz)]

    for d in (1, 3, 2):
        arrived(block_at(0, d, 0), wr.at[0, d, 0])
        for e in RING:
            sent.append(to(0, d, e, 0, e))
        arrived(block_at(1, 0, d), wr.at[1, 0, d])
        for e in RING:
            sent.append(to(1, e, d, e, 0))

    e_loc.wait()
    e_sib.wait()
    q_loc.wait()
    for dxh in range(2):
        for dz in range(4):
            if dxh or dz:
                src = ((xh + dxh) % 2) * 4 + mod4(z - dz)
                arrived(qb.at[src], qrecv.at[dxh, dz])

    def prepare(b, _):
        block = qb[b, 0:256, :]
        low = lanes_of((256, 128)) < 64
        zero = jnp.zeros_like(block)
        xs[b, 0:256, :] = jnp.where(low, block, zero)
        xs[b, 256:512, :] = jnp.where(low, zero, block)
        turned = block.T
        xt[b, 0:64, 0:256] = turned[0:64] * jnp.asarray(0.125, BF)
        xt[b, 64:128, 256:512] = turned[64:128]
        xt[b, 0:64, 256:512] = jnp.zeros((64, 256), BF)
        xt[b, 64:128, 0:256] = jnp.zeros((64, 256), BF)
        xt[b, 128:256, :] = jnp.zeros((128, 512), BF)
        ids = qb[b, 256:272, :].astype(F32)
        ids = jnp.concatenate([ids[0:1], ids[1:2]], axis=1)
        row = lax.broadcasted_iota(jnp.int32, (16, 256), 0)
        differs = (row < 4) & (row.astype(F32) != ids)
        xt[b, 128:144, 0:256] = jnp.where(differs, NEG, 0.0).astype(BF)
        dec_out[b] = jnp.broadcast_to(ids, (8, 256))
        return 0

    lax.fori_loop(0, 8, prepare, 0)

    def one_hot(i, _):
        seg = eseg[pl.ds(i, 1), :].astype(F32)
        row = lax.broadcasted_iota(jnp.int32, (128, 128), 0).astype(F32)
        hot = jnp.where(row == seg, 1.0, 0.0)
        kvx[pl.ds(pl.multiple_of(i * 128, 128), 128), 128:256] = hot.T.astype(BF)
        return 0

    lax.fori_loop(0, 32, one_hot, 0)

    def multiply(a, dx, dz, first):
        bx, bz = mod4(x - dx), mod4(z - dz)
        columns = pl.ds(pl.multiple_of((row_group(bx) * 4 + bz) * 256, 256), 256)
        for half in range(2):
            term = jnp.dot(encv[half, :, columns], wg[a, row_group(bx), bz], preferred_element_type=F32)
            if first:
                acc[a, pl.ds(half * 256, 256), :] = term
            else:
                acc[a, pl.ds(half * 256, 256), :] += term

    multiply(0, 0, 0, True)
    multiply(1, 0, 0, True)
    for d in (1, 3, 2):
        multiply(0, d, 0, False)
        multiply(1, 0, d, False)
    for d in (1, 3, 2):
        arrived(block_at(0, 0, d), wr.at[0, 0, d])
        multiply(0, 0, d, False)
        arrived(block_at(1, d, 0), wr.at[1, d, 0])
        multiply(1, d, 0, False)
    for d in (1, 3, 2):
        for e in (1, 3, 2):
            arrived(block_at(0, d, e), wr.at[0, d, e])
            multiply(0, d, e, False)
            arrived(block_at(1, e, d), wr.at[1, e, d])
            multiply(1, e, d, False)

    for j in range(4):
        tile = pl.ds((j // 2) * 128, 128)
        odd = j % 2 == 1
        kvs[j] = halves(acc[0, :, tile], acc[1, :, tile], odd, not odd).astype(BF)

    w_save = pltpu.make_async_copy(wg, wg_out, loc.at[3])
    w_save.start()
    ex = (c + 2 - xh) % 2
    tx = c * 2 + x % 2
    here = c == xh

    def kv_copy(dz, dc):
        hz = mod4(z + dz)
        return remote(
            kvs.at[hz], kvb.at[t], ksend.at[dz, dc], krecv.at[ex, dz], dev(tx, hz, (c + dc) % 2, y)
        )

    kv_loc = pltpu.make_async_copy(kvs.at[z], kvb.at[t], loc.at[4])
    k_sent = [kv_copy(dz, dc) for dz in (2, 1, 3) for dc in range(2)]
    for copy in k_sent:
        copy.start()
    kv_copy(0, 1).start()

    @pl.when(here)
    def _():
        kv_loc.start()

    @pl.when(jnp.logical_not(here))
    def _():
        kv_copy(0, 0).start()

    for e in (0, 1):
        for dz in (0, 1, 3, 2):
            src = ((xh + e) % 2) * 4 + mod4(z - dz)
            if e == 0 and dz == 0:

                @pl.when(here)
                def _():
                    kv_loc.wait()

                @pl.when(jnp.logical_not(here))
                def _():
                    arrived(kvb.at[t], krecv.at[0, 0])
            else:
                arrived(kvb.at[src], krecv.at[e, dz])
            block = kvb[src]
            span = pl.ds(pl.multiple_of(src * 512, 512), 512)
            kvx[span, 0:128] = block
            kvt[:, span] = block.T

    for copy in sent + q_sent + k_sent:
        copy.wait_send()
    kv_copy(0, 1).wait_send()

    @pl.when(jnp.logical_not(here))
    def _():
        kv_copy(0, 0).wait_send()

    w_save.wait()


def attend(kvx, kvt, xt, xs, dec, eseg, dkv_out, dq_out, tt, yy, dkv):
    dkv[...] = jnp.zeros_like(dkv)
    seg = eseg[...].astype(F32)

    def one_block(b, _):
        ids = dec[b]
        low, high = jnp.min(ids), jnp.max(ids)
        begin = jnp.sum(jnp.where(seg < low, 1.0, 0.0)).astype(jnp.int32)
        end = jnp.sum(jnp.where(seg <= high, 1.0, 0.0)).astype(jnp.int32)
        j0, j1 = begin // KB, (end + KB - 1) // KB

        def at(j):
            return pl.ds(pl.multiple_of(j * KB, KB), KB)

        def fold(op, v):
            return op(v.reshape(KB // 8, 8, 256), axis=0)

        def scores(j, top):
            both = jnp.dot(kvx[at(j), :], xt[b], preferred_element_type=F32)
            tt[at(j), :] = both
            return jnp.maximum(top, fold(jnp.max, both[:, 0:256]))

        top = lax.fori_loop(j0, j1, scores, jnp.full((8, 256), -3e38, F32))
        top = jnp.max(top, axis=0, keepdims=True)

        def weigh(j, total):
            e = jnp.exp(tt[at(j), 0:256] - top)
            tt[at(j), 0:256] = e
            return total + fold(jnp.sum, e)

        total = lax.fori_loop(j0, j1, weigh, jnp.zeros((8, 256), F32))
        inv = 1.0 / jnp.sum(total, axis=0, keepdims=True)

        def deltas(j, delta):
            low_p = (tt[at(j), 0:256] * inv).astype(BF)
            yy[at(j), 256:512] = low_p
            return delta + fold(jnp.sum, low_p.astype(F32) * tt[at(j), 256:512])

        delta = lax.fori_loop(j0, j1, deltas, jnp.zeros((8, 256), F32))
        delta = jnp.sum(delta, axis=0, keepdims=True)
        inv8 = inv * 0.125

        def grads(j, dq):
            ds = ((tt[at(j), 0:256] * inv8) * (tt[at(j), 256:512] - delta)).astype(BF)
            yy[at(j), 0:256] = ds
            dkv[at(j), :] += jnp.dot(yy[at(j), :], xs[b], preferred_element_type=F32)
            return dq + jnp.dot(kvt[0:64, at(j)], ds, preferred_element_type=F32)

        dq = lax.fori_loop(j0, j1, grads, jnp.zeros((64, 256), F32))
        dq_out[b] = jnp.concatenate([dq[:, 0:128], dq[:, 128:256]], axis=0).T.astype(BF)
        return 0

    lax.fori_loop(0, 8, one_block, 0)
    dkv_out[...] = dkv[...].astype(BF).reshape(dkv_out.shape)


def back(
    dkvp, dqp, enc, w,
    enc_out, q_out, w_out,
    encv, wv, rb, gt, gs, qg, sa, ra, s2, r2, oa, ys, yr, fin, fsib,
    loc, sib_s, sib_r, dsend, drecv, qsend, qrecv, asend, arecv, bsend, brecv, ysend, yrecv,
):
    x, xh, z, c, y = coords()
    me = row_group(x)
    sibling = dev(x, z, 1 - c, y)
    peers = [sibling]
    for dx in range(4):
        for dz in range(4):
            if dx == 0 and dz == 0:
                continue
            if dx in (0, 2) or dz == 0:
                peers.append(dev(mod4(x + dx), mod4(z + dz), c, y))
            if dx in (0, 2):
                peers.append(dev(mod4(x + dx), mod4(z + dz), 1 - c, y))
    for dy in range(1, 4):
        peers.append(dev(x, z, c, mod4(y + dy)))
    greet(peers)

    here = c == xh

    def d_copy(dxh, dz):
        tx, tz = (xh + dxh) % 2, mod4(z + dz)
        return remote(
            dkvp.at[tx * 4 + tz], rb.at[z, c], dsend.at[dxh, dz], drecv.at[dz, c],
            dev(tx * 2 + x % 2, tz, xh, y),
        )

    d_sent = [d_copy(dxh, dz) for dxh in (1, 0) for dz in (2, 1, 3, 0) if dxh or dz]
    for copy in d_sent:
        copy.start()
    d_loc = pltpu.make_async_copy(dkvp.at[xh * 4 + z], rb.at[z, c], loc.at[0])

    @pl.when(here)
    def _():
        d_loc.start()

    @pl.when(jnp.logical_not(here))
    def _():
        d_copy(0, 0).start()

    e_sib = remote(enc, encv.at[c], sib_s.at[0], sib_r.at[0], sibling)
    e_sib.start()
    e_loc = pltpu.make_async_copy(enc, encv.at[c], loc.at[1])
    e_loc.start()
    w_sib = remote(w, wv.at[c], sib_s.at[1], sib_r.at[1], sibling)
    w_sib.start()
    w_loc = pltpu.make_async_copy(w, wv.at[c], loc.at[2])
    w_loc.start()
    q_sent = []
    for dxh in (1, 0):
        for dz in (2, 1, 3, 0):
            if dxh or dz:
                tx, tz = (xh + dxh) % 2, mod4(z + dz)
                copy = remote(
                    dqp.at[tx * 4 + tz], qg.at[xh * 4 + z], qsend.at[dxh, dz], qrecv.at[dxh, dz],
                    dev(tx * 2 + x % 2, tz, c, y),
                )
                copy.start()
                q_sent.append(copy)
    q_loc = pltpu.make_async_copy(dqp.at[xh * 4 + z], qg.at[xh * 4 + z], loc.at[3])
    q_loc.start()

    for dz in (0, 1, 3, 2):
        j = mod4(z - dz)
        for s in range(2):
            if dz == 0:
                local = jnp.logical_and(here, c == s)

                @pl.when(local)
                def _():
                    d_loc.wait()

                @pl.when(jnp.logical_not(local))
                def _():
                    arrived(rb.at[j, s], drecv.at[0, s])
            else:
                arrived(rb.at[j, s], drecv.at[dz, s])
        turned = (rb[j, 0].astype(F32) + rb[j, 1].astype(F32)).astype(BF).T
        keys = pl.ds(pl.multiple_of(j * 64, 64), 64)
        gt[0, keys, :] = turned[0:64]
        gt[1, keys, :] = turned[64:128]

    own_tok = pl.ds(pl.multiple_of(c * 256, 256), 256)
    sib_tok = pl.ds(pl.multiple_of((1 - c) * 256, 256), 256)
    g_sib = remote(gt.at[:, :, sib_tok], gs.at[c], sib_s.at[2], sib_r.at[2], sibling)
    g_sib.start()
    gs_own = pltpu.make_async_copy(gt.at[:, :, own_tok], gs.at[c], loc.at[4])
    gs_own.start()
    e_loc.wait()
    e_sib.wait()

    def product(a, dx, dz):
        bx, bz = mod4(x + dx), mod4(z + dz)
        columns = pl.ds(pl.multiple_of((row_group(bx) * 4 + bz) * 256, 256), 256)
        return jnp.dot(gt[a, :, 0:256], encv[0, :, columns], preferred_element_type=F32) + jnp.dot(
            gt[a, :, 256:512], encv[1, :, columns], preferred_element_type=F32
        )

    a_sent = []

    def first_hop(far):
        for d in RING:
            for a in range(2):
                dx, dz = (far, d) if a == 0 else (d, far)
                sa[a, d - 1, far] = product(a, dx, dz).astype(BF)
                step_x, step_z = (0, d) if a == 0 else (d, 0)
                copy = remote(
                    sa.at[a, d - 1, far], ra.at[a, d - 1, far], asend.at[a, d - 1, far], arecv.at[a, d - 1, far],
                    dev(mod4(x + step_x), mod4(z + step_z), c, y),
                )
                copy.start()
                a_sent.append(copy)

    def enc_term(dy, r):
        group = mod4(y + dy)
        total = None
        for half in range(2):
            for a in range(2):
                term = jnp.dot(wv[half, a, group, r], gs[half, a], preferred_element_type=F32)
                total = term if total is None else total + term
        return total

    y_sent = []

    def to_group(dy):
        for r in range(4):
            ys[dy - 1, pl.ds(r * 256, 256), :] = enc_term(dy, r).astype(BF)
        copy = remote(
            ys.at[dy - 1], yr.at[dy - 1], ysend.at[dy - 1], yrecv.at[dy - 1], dev(x, z, c, mod4(y + dy))
        )
        copy.start()
        y_sent.append(copy)

    first_hop(2)
    w_loc.wait()
    w_sib.wait()
    gs_own.wait()
    g_sib.wait()
    to_group(2)
    first_hop(1)
    to_group(1)
    first_hop(3)
    to_group(3)
    first_hop(0)
    for far in (2, 1, 3, 0):
        for a in range(2):
            dx, dz = (far, 0) if a == 0 else (0, far)
            oa[a, far] = product(a, dx, dz)

    b_sent = []
    for far in (2, 1, 3, 0):
        for a in range(2):
            total = oa[a, far]
            for d in RING:
                arrived(ra.at[a, d - 1, far], arecv.at[a, d - 1, far])
                total = total + ra[a, d - 1, far].astype(F32)
            if far == 0:
                oa[a, 0] = total
            else:
                s2[a, far - 1] = total.astype(BF)
                step_x, step_z = (far, 0) if a == 0 else (0, far)
                copy = remote(
                    s2.at[a, far - 1], r2.at[a, far - 1], bsend.at[a, far - 1], brecv.at[a, far - 1],
                    dev(mod4(x + step_x), mod4(z + step_z), c, y),
                )
                copy.start()
                b_sent.append(copy)

    q_loc.wait()
    for dxh in range(2):
        for dz in range(4):
            if dxh or dz:
                src = ((xh + dxh) % 2) * 4 + mod4(z - dz)
                arrived(qg.at[src], qrecv.at[dxh, dz])
    for i in range(4):
        tile = pl.ds(i * 128, 128)
        even, odd = qg[2 * i].astype(F32), qg[2 * i + 1].astype(F32)
        q_out[0:128, tile] = halves(even, odd, False, True).astype(BF)
        q_out[128:256, tile] = halves(even, odd, True, False).astype(BF)

    for a in range(2):
        total = oa[a, 0]
        for d in RING:
            arrived(r2.at[a, d - 1], brecv.at[a, d - 1])
            total = total + r2[a, d - 1].astype(F32)
        fin[a] = total
    mine = pl.ds(pl.multiple_of(c * 128, 128), 128)
    theirs = pl.ds(pl.multiple_of((1 - c) * 128, 128), 128)
    f_sib = remote(fin.at[:, :, theirs], fsib.at[c], sib_s.at[3], sib_r.at[3], sibling)
    f_sib.start()
    w_out[:, pl.ds(pl.multiple_of(c * 256, 256), 256), :] = fin[:, :, mine]

    for r in range(4):
        part = pl.ds(r * 256, 256)
        total = enc_term(0, r).astype(BF).astype(F32)
        if r == 0:
            for dy in RING:
                arrived(yr.at[dy - 1], yrecv.at[dy - 1])
        for dy in RING:
            total = total + yr[dy - 1, part, :].astype(F32)
        enc_out[part, :] = total.astype(BF)

    f_sib.wait()
    w_out[:, pl.ds(pl.multiple_of((1 - c) * 256, 256), 256), :] = fsib[1 - c]

    for copy in d_sent + q_sent + a_sent + b_sent + y_sent:
        copy.wait_send()

    @pl.when(jnp.logical_not(here))
    def _():
        d_copy(0, 0).wait_send()


VM = pl.BlockSpec(memory_space=pltpu.VMEM)
ANY = pl.BlockSpec(memory_space=pl.ANY)
DMA = pltpu.SemaphoreType.DMA


def params(collective_id=None):
    if collective_id is None:
        return pltpu.CompilerParams(vmem_limit_bytes=60 << 20)
    return pltpu.CompilerParams(
        collective_id=collective_id, has_side_effects=True, vmem_limit_bytes=60 << 20
    )


def body(enc_out, dec_query, ctx_grad, kv_weight, enc_seg, dec_seg):
    enc = enc_out[0]
    eseg = enc_seg.reshape(32, 128)
    dseg = jnp.pad(dec_seg.reshape(2, 128), ((0, 14), (0, 0)))
    shape = jax.ShapeDtypeStruct
    wg, kvx, kvt, xt, xs, dec = pl.pallas_call(
        front,
        out_shape=(
            shape((2, 4, 4, 256, 256), BF),
            shape((4096, 256), BF),
            shape((128, 4096), BF),
            shape((8, 256, 512), BF),
            shape((8, 512, 128), BF),
            shape((8, 8, 256), F32),
        ),
        in_specs=[ANY, VM, VM, ANY, VM, VM],
        out_specs=(ANY, VM, VM, VM, VM, VM),
        scratch_shapes=[
            pltpu.VMEM((2, 256, 4096), BF),
            pltpu.VMEM((2, 4, 4, 256, 256), BF),
            pltpu.VMEM((2, 512, 256), F32),
            pltpu.VMEM((4, 512, 128), BF),
            pltpu.VMEM((8, 512, 128), BF),
            pltpu.VMEM((8, 272, 128), BF),
            pltpu.VMEM((8, 272, 128), BF),
            DMA((5,)), DMA((2,)), DMA((2,)),
            DMA((2, 4, 4)), DMA((2, 4, 4)),
            DMA((2, 4)), DMA((2, 4)),
            DMA((4, 2)), DMA((2, 4)),
        ],
        compiler_params=params(1),
        name="front",
    )(enc, dec_query[0], ctx_grad[0], kv_weight, dseg, eseg)

    dkvp, dqp = pl.pallas_call(
        attend,
        out_shape=(shape((8, 512, 128), BF), shape((8, 128, 128), BF)),
        in_specs=[VM] * 6,
        out_specs=(VM, VM),
        scratch_shapes=[
            pltpu.VMEM((4096, 512), F32),
            pltpu.VMEM((4096, 512), BF),
            pltpu.VMEM((4096, 128), F32),
        ],
        compiler_params=params(),
        name="attend",
    )(kvx, kvt, xt, xs, dec, eseg)

    enc_t, q_grad, w_t = pl.pallas_call(
        back,
        out_shape=(shape((1024, 256), BF), shape((256, 512), BF), shape((2, 512, 128), F32)),
        in_specs=[ANY, ANY, ANY, ANY],
        out_specs=(VM, VM, VM),
        scratch_shapes=[
            pltpu.VMEM((2, 256, 4096), BF),
            pltpu.VMEM((2, 2, 4, 4, 256, 256), BF),
            pltpu.VMEM((4, 2, 512, 128), BF),
            pltpu.VMEM((2, 256, 512), BF),
            pltpu.VMEM((2, 2, 256, 256), BF),
            pltpu.VMEM((8, 128, 128), BF),
            pltpu.VMEM((2, 3, 4, 256, 256), BF),
            pltpu.VMEM((2, 3, 4, 256, 256), BF),
            pltpu.VMEM((2, 3, 256, 256), BF),
            pltpu.VMEM((2, 3, 256, 256), BF),
            pltpu.VMEM((2, 4, 256, 256), F32),
            pltpu.VMEM((3, 1024, 256), BF),
            pltpu.VMEM((3, 1024, 256), BF),
            pltpu.VMEM((2, 256, 256), F32),
            pltpu.VMEM((2, 2, 256, 128), F32),
            DMA((5,)), DMA((4,)), DMA((4,)),
            DMA((2, 4)), DMA((4, 2)),
            DMA((2, 4)), DMA((2, 4)),
            DMA((2, 3, 4)), DMA((2, 3, 4)),
            DMA((2, 3)), DMA((2, 3)),
            DMA((3,)), DMA((3,)),
        ],
        compiler_params=params(2),
        name="back",
    )(dkvp, dqp, enc, wg)
    return enc_t.T[None], q_grad[None], w_t.transpose(0, 2, 1)


def solution(mesh):
    placed = (
        P("dp", "seq", None),
        P("dp", "seq", "mp"),
        P("dp", "seq", "mp"),
        P(None, ("dp", "seq"), "mp"),
        P("dp", None),
        P("dp", "seq"),
    )
    return jax.shard_map(
        body,
        mesh=mesh,
        in_specs=placed,
        out_specs=(P("dp", "seq", "mp"), P("dp", "seq", "mp"), P(None, ("dp", "seq"), "mp")),
        check_vma=False,
    )
```

time: 624 us -> 156 us (0.25)
  waiting for transfers between devices: 433 us -> 0 us
  Pallas kernels: 0 us -> 149 us
  matrix products: 120 us -> 0 us
  local copies, waits for them, and re-layouts: 41.1 us -> 6.11 us
  between operations: 13.9 us -> 0.66 us
  other arithmetic: 13.2 us -> 0 us
    all_gather x2 -> x0, waiting for transfers between devices: 166 us -> none  [the longest x1 89.5 us: body(): full_weight = lax.all_gather(kv_weight, ('dp', 'seq'), axis=1, tiled=True)]
    pallas_call x0 -> x3, Pallas kernels: none -> 149 us  [the longest x1 65.8 us: body(): pl.pallas_call(front, out_shape=(shape((2, 4, 4, 256, 256), BF), shape((4...]
    reduce_scatter x2 -> x0, waiting for transfers between devices: 135 us -> none  [the longest x1 98.4 us: body(): lax.psum_scatter(key_terms, 'seq', scatter_dimension=1, tiled=True)]
    unnamed x6 -> x0, waiting for transfers between devices: 131 us -> none
    dot_general x51 -> x0, matrix products: 120 us -> none  [the longest x8 22.3 us: head_backward(): dprobs = jnp.dot(grad_out, values.T, preferred_element_type=jnp.float32)]
    another operation x2 -> x0, local copies, waits for them, and re-layouts: 16.9 us -> none  [split_heads(): return array.reshape(array.shape[0], head_count, DH).transpose(1, 0, 2)]
    unnamed x19 -> x5, local copies, waits for them, and re-layouts: 18.1 us -> 4.83 us
    another operation x3 -> x0, other arithmetic: 7.46 us -> none  [the longest x1 7.46 us: body(): jnp.stack([join_heads(dkeys).astype(jnp.bfloat16), join_heads(dvalues).as...]
  transfers between devices with their start and end apart: 5 -> 0, of which waited for: 5 -> 0; matrix products, arithmetic and copies ran while one was open for 2% -> 0% of each run, Pallas kernels for 0% -> 0%
where the time goes in v1:
time: 156 us
  Pallas kernels  149 us (96%)
  local copies, waits for them, and re-layouts  6.11 us (4%)
    pallas_call x1, Pallas kernels, body(): pl.pallas_call(front, out_shape=(shape((2, 4, 4, 256, 256), BF), shape((4...  65.8 us
    pallas_call x1, Pallas kernels, body(): pl.pallas_call(back, out_shape=(shape((1024, 256), BF), shape((256, 512),...  52.6 us
    pallas_call x1, Pallas kernels, body(): pl.pallas_call(attend, out_shape=(shape((8, 512, 128), BF), shape((8, 128...  30.9 us
    unnamed x5, local copies, waits for them, and re-layouts  4.83 us

profile of v1, /device:TPU:1, one launch (start us, length us, event | category | flops | bytes accessed | tf_op | source)
XLA Modules:
  0.0 156.1 jit_solution(2942055744474686805)
XLA Ops:
  0.6 1.3 pad.4.dseg
  1.9 65.8 %front.1 = (bf16[2,4,4,256,256]{4,3,2,1,0:T(8,128)(2,1)}, bf16[4096,256]{1,0:T(8,128)(2,1)}, bf16[128,4096]{1,0:T(8,128)(2,1)}, bf16[8,256,512]{2,1,0:T(8,128)(2...) custom-call(bf16[256,4096]{1,0:T(8,128)(2,1)} %bitcast.10, bf16[256,512]{1,0:T(8,128)(2,1)} %bitcast.15, ...), custom_call_target="tpu_custom_call" | custom-call | tf_op jit(solution)/shard_map/front/pallas_call | solution.py:565
  67.8 30.9 %attend.1 = (bf16[8,512,128]{2,1,0:T(8,128)(2,1)}, bf16[8,128,128]{2,1,0:T(8,128)(2,1)}) custom-call(bf16[4096,256]{1,0:T(8,128)(2,1)} %get-tuple-element.14.kvx, bf16[128,4096]{1,0:T(8,128)(2,1)} %get-tuple-element.15.kvt, bf16[8,256,512]{2,1,0:T(8,128)(2,1)} %get-tuple-element.16.xt, bf16[8,512,128]{2,1,0:T(8,128)(2,1)} %get-tuple-element.17.xs, ...), custom_call_target="tpu_custom_call" | custom-call | tf_op jit(solution)/shard_map/attend/pallas_call | solution.py:594
  98.7 52.6 %back.1 = (bf16[1024,256]{1,0:T(8,128)(2,1)}, bf16[256,512]{1,0:T(8,128)(2,1)}, f32[2,512,128]{2,1,0:T(8,128)}) custom-call(bf16[8,512,128]{2,1,0:T(8,128)(2,1)} %get-tuple-element.19.dkvp, bf16[8,128,128]{2,1,0:T(8,128)(2,1)} %get-tuple-element.20.dqp, bf16[256,4096]{1,0:T(8,128)(2,1)} %bitcast.11, bf16[2,4,4,256,256]{4,3,2,1,0:T(8,128)(2,1)} %get-tuple-element.21.w), custom_call_target="tpu_custom_call" | custom-call | tf_op jit(solution)/shard_map/back/pallas_call | solution.py:608
  151.3 0.0 copy-start
  151.3 2.1 %copy.9 = bf16[1,256,1024]{2,1,0:T(8,128)(2,1)} copy(bf16[1,256,1024]{1,2,0:T(8,128)(2,1)} %bitcast.13) | data formatting | bytes 1048576
  153.4 2.0 %copy.10 = f32[2,128,512]{2,1,0:T(8,128)} copy(f32[2,128,512]{1,2,0:T(8,128)} %bitcast.12) | data formatting | bytes 1048576
  155.4 0.0 copy-done
  155.4 0.7 copy.12
Async XLA Ops:
  151.3 4.1 %copy-start = (bf16[256,512]{1,0:T(8,128)(2,1)S(1)}, bf16[256,512]{1,0:T(8,128)(2,1)}, u32[]{:S(2)}) copy-start(bf16[256,512]{1,0:T(8,128)(2,1)} %get-tuple-element.23) | copy-start | bytes 786436

commit v2 on v1

v2 whole, which is shorter than its diff:
```python
import functools

import jax
import jax.numpy as jnp
from jax import lax
from jax.experimental import pallas as pl
from jax.experimental.pallas import tpu as pltpu
from jax.sharding import PartitionSpec as P

MESH = pl.DeviceIdType.MESH
BF = jnp.bfloat16
F32 = jnp.float32
NEG = -1e30
KB = 512


def coords():
    dp, seq, y = lax.axis_index("dp"), lax.axis_index("seq"), lax.axis_index("mp")
    xh = seq // 8
    return xh * 2 + dp, xh, (seq // 2) % 4, seq % 2, y


def dev(x, z, core, y):
    return (x % 2, (x // 2) * 8 + z * 2 + core, y)


def row_group(x):
    return (x % 2) * 2 + x // 2


def mod4(v):
    return (v + 4) % 4


def remote(src, dst, send, recv, device):
    return pltpu.make_async_remote_copy(
        src_ref=src, dst_ref=dst, send_sem=send, recv_sem=recv, device_id=device, device_id_type=MESH
    )


def arrived(dst, sem):
    pltpu.make_async_copy(dst, dst, sem).wait()


def greet(peers):
    for peer in peers:
        pl.semaphore_signal(pltpu.get_barrier_semaphore(), inc=1, device_id=peer, device_id_type=MESH)


def greeted(peers):
    pl.semaphore_wait(pltpu.get_barrier_semaphore(), len(peers))


def plane_peers(x, z, c, y):
    peers = [dev(x, z, 1 - c, y), dev(mod4(x + 1), z, c, y), dev(mod4(x + 3), z, c, y)]
    for dx in (0, 2):
        for dz in range(4):
            if dx or dz:
                peers += [dev(mod4(x + dx), mod4(z + dz), core, y) for core in range(2)]
    return peers


def lanes_of(shape):
    return lax.broadcasted_iota(jnp.int32, shape, 1)


def halves(first, second, shift_first, shift_second):
    first = pltpu.roll(first, 64, 1) if shift_first else first
    second = pltpu.roll(second, 64, 1) if shift_second else second
    return jnp.where(lanes_of(first.shape) < 64, first, second)


def front(
    enc, q, do, w, dseg, eseg,
    wg_out, kvx, kvt, xt, xs, dec_out,
    encv, wg, acc, kvs, kvb, qs, qb,
    loc, sib_s, sib_r, ws, wr, qsend, qrecv, ksend, krecv, fsend, frecv,
):
    x, xh, z, c, y = coords()
    me = row_group(x)
    t = xh * 4 + z
    sibling = dev(x, z, 1 - c, y)
    peers = plane_peers(x, z, c, y)
    greet(peers)

    own = pl.multiple_of(c * 256, 256)
    other = pl.multiple_of((1 - c) * 256, 256)
    rows = pl.ds(pl.multiple_of(c * 128, 128), 128)
    w_loc = pltpu.make_async_copy(w.at[:, :, pl.ds(own, 256)], wg.at[:, me, z, rows], loc.at[0])
    w_loc.start()
    e_loc = pltpu.make_async_copy(enc, encv.at[c], loc.at[1])
    e_loc.start()

    ids = dseg[...].astype(F32)
    row = lax.broadcasted_iota(jnp.int32, (16, 128), 0)
    id_rows = jnp.where(row == 0, ids[0:1], jnp.where(row == 1, ids[1:2], 0.0)).astype(BF)
    for h in range(8):
        tile = pl.ds((h // 2) * 128, 128)
        odd = h % 2 == 1
        qs[h, 0:256, :] = halves(q[:, tile].astype(F32), do[:, tile].astype(F32), odd, not odd).astype(BF)
        qs[h, 256:272, :] = id_rows
    q_loc = pltpu.make_async_copy(qs.at[t], qb.at[t], loc.at[2])
    q_loc.start()
    greeted(peers)

    w_sib = remote(w.at[:, :, pl.ds(other, 256)], wg.at[:, me, z, rows], sib_s.at[0], sib_r.at[0], sibling)
    w_sib.start()
    q_sent = []
    for dxh in (1, 0):
        for dz in (2, 1, 3, 0):
            if dxh == 0 and dz == 0:
                continue
            hx, hz = (xh + dxh) % 2, mod4(z + dz)
            copy = remote(
                qs.at[hx * 4 + hz], qb.at[t], qsend.at[dxh, dz], qrecv.at[dxh, dz],
                dev(mod4(x + 2 * dxh), hz, c, y),
            )
            copy.start()
            q_sent.append(copy)
    e_sib = remote(enc, encv.at[c], sib_s.at[1], sib_r.at[1], sibling)
    e_sib.start()
    w_loc.wait()
    w_sib.wait()

    def place(a, first, second):
        bx, bz = (first, second) if a == 0 else (second, first)
        return row_group(mod4(x - bx)), mod4(z - bz)

    def block_of(a, first, second, half=None):
        group, bz = place(a, first, second)
        block = wg.at[a, group, bz]
        return block if half is None else block.at[pl.ds(half * 128, 128)]

    sent = []

    def pass_on(a, first, second, ring, step, half=None):
        block = block_of(a, first, second, half)
        to_first, to_second = (first + step) % 4 if ring == 0 else first, (second + step) % 4 if ring else second
        sem = (a, to_first, to_second, half or 0)
        along_x = (a == 0) == (ring == 0)
        target = dev(mod4(x + step), z, c, y) if along_x else dev(x, mod4(z + step), c, y)
        copy = remote(block, block, ws.at[sem], wr.at[sem], target)
        copy.start()
        sent.append(copy)

    def take(a, first, second):
        if second == 2 or (first == 2 and second == 0):
            for half in range(2):
                arrived(block_of(a, first, second, half), wr.at[a, first, second, half])
        else:
            arrived(block_of(a, first, second), wr.at[a, first, second, 0])

    def multiply(a, first, second, fresh=False):
        group, bz = place(a, first, second)
        columns = pl.ds(pl.multiple_of((group * 4 + bz) * 256, 256), 256)
        for half in range(2):
            term = jnp.dot(encv[half, :, columns], wg[a, group, bz], preferred_element_type=F32)
            if fresh:
                acc[a, pl.ds(half * 256, 256), :] = term
            else:
                acc[a, pl.ds(half * 256, 256), :] += term

    def both_ways(a, first):
        pass_on(a, first, 0, 1, 1)
        pass_on(a, first, 0, 1, -1)

    for step in (1, -1):
        for a in range(2):
            pass_on(a, 0, 0, 0, step)
    for a in range(2):
        both_ways(a, 0)

    def one_hot(i, _):
        seg = eseg[pl.ds(i, 1), :].astype(F32)
        row = lax.broadcasted_iota(jnp.int32, (128, 128), 0).astype(F32)
        hot = jnp.where(row == seg, 1.0, 0.0)
        kvx[pl.ds(pl.multiple_of(i * 128, 128), 128), 128:256] = hot.T.astype(BF)
        return 0

    lax.fori_loop(0, 32, one_hot, 0)

    for a in range(2):
        take(a, 1, 0)
        pass_on(a, 1, 0, 0, 1, 0)
        take(a, 3, 0)
        pass_on(a, 3, 0, 0, -1, 1)
    for a in range(2):
        both_ways(a, 1)
        both_ways(a, 3)
    for a in range(2):
        take(a, 0, 1)
        pass_on(a, 0, 1, 1, 1, 0)
        take(a, 0, 3)
        pass_on(a, 0, 3, 1, -1, 1)
    for a in range(2):
        take(a, 2, 0)
        both_ways(a, 2)
    e_loc.wait()
    e_sib.wait()
    for a in range(2):
        multiply(a, 0, 0, True)
        for first, second in ((1, 0), (3, 0), (0, 1), (0, 3), (2, 0)):
            multiply(a, first, second)

    q_loc.wait()
    for dxh in range(2):
        for dz in range(4):
            if dxh or dz:
                src = ((xh + dxh) % 2) * 4 + mod4(z - dz)
                arrived(qb.at[src], qrecv.at[dxh, dz])

    def prepare(b, _):
        block = qb[b, 0:256, :]
        low = lanes_of((256, 128)) < 64
        zero = jnp.zeros_like(block)
        xs[b, 0:256, :] = jnp.where(low, block, zero)
        xs[b, 256:512, :] = jnp.where(low, zero, block)
        turned = block.T
        xt[b, 0:64, 0:256] = turned[0:64] * jnp.asarray(0.125, BF)
        xt[b, 64:128, 256:512] = turned[64:128]
        xt[b, 0:64, 256:512] = jnp.zeros((64, 256), BF)
        xt[b, 64:128, 0:256] = jnp.zeros((64, 256), BF)
        xt[b, 128:256, :] = jnp.zeros((128, 512), BF)
        ids = qb[b, 256:272, :].astype(F32)
        ids = jnp.concatenate([ids[0:1], ids[1:2]], axis=1)
        row = lax.broadcasted_iota(jnp.int32, (16, 256), 0)
        differs = (row < 4) & (row.astype(F32) != ids)
        xt[b, 128:144, 0:256] = jnp.where(differs, NEG, 0.0).astype(BF)
        dec_out[b] = jnp.broadcast_to(ids, (8, 256))
        return 0

    for first in (1, 3, 2):
        for a in range(2):
            take(a, first, 1)
            pass_on(a, first, 1, 1, 1, 0)
            take(a, first, 3)
            pass_on(a, first, 3, 1, -1, 1)
            multiply(a, first, 1)
            multiply(a, first, 3)
        if first != 2:
            lax.fori_loop(0 if first == 1 else 4, 4 if first == 1 else 8, prepare, 0)
    for first in (0, 1, 3, 2):
        for a in range(2):
            take(a, first, 2)
            multiply(a, first, 2)

    for j in range(4):
        tile = pl.ds((j // 2) * 128, 128)
        odd = j % 2 == 1
        kvs[j] = halves(acc[0, :, tile], acc[1, :, tile], odd, not odd).astype(BF)

    ex = (c + 2 - xh) % 2
    tx = c * 2 + x % 2
    here = c == xh

    def kv_copy(dz, core):
        hz = mod4(z + dz)
        part = pl.ds(core * 256, 256)
        return remote(
            kvs.at[hz, part], kvb.at[t, part], ksend.at[dz, core], krecv.at[ex, dz], dev(tx, hz, core, y)
        )

    def kv_local(core):
        part = pl.ds(core * 256, 256)
        return pltpu.make_async_copy(kvs.at[z, part], kvb.at[t, part], loc.at[4])

    k_sent = [kv_copy(dz, core) for dz in (2, 1, 3) for core in range(2)]
    for copy in k_sent:
        copy.start()
    for core in range(2):
        local = jnp.logical_and(here, c == core)

        @pl.when(local)
        def _():
            kv_local(core).start()

        @pl.when(jnp.logical_not(local))
        def _():
            kv_copy(0, core).start()

    w_save = pltpu.make_async_copy(wg, wg_out, loc.at[3])
    w_save.start()

    mine = pl.ds(pl.multiple_of(c * 256, 256), 256)
    theirs = pl.ds(pl.multiple_of((1 - c) * 256, 256), 256)

    def source(e, dz):
        return ((xh + e) % 2) * 4 + mod4(z - dz)

    f_sent = []

    def hand_over(e, dz):
        src = source(e, dz)
        if e == 0 and dz == 0:

            @pl.when(here)
            def _():
                for core in range(2):

                    @pl.when(c == core)
                    def _():
                        kv_local(core).wait()

            @pl.when(jnp.logical_not(here))
            def _():
                arrived(kvb.at[src, mine], krecv.at[0, 0])
        else:
            arrived(kvb.at[src, mine], krecv.at[e, dz])
        copy = remote(kvb.at[src, mine], kvb.at[src, mine], fsend.at[e, dz], frecv.at[e, dz], sibling)
        copy.start()
        f_sent.append(copy)

    def use(e, dz):
        src = source(e, dz)
        arrived(kvb.at[src, theirs], frecv.at[e, dz])
        block = kvb[src]
        span = pl.ds(pl.multiple_of(src * 512, 512), 512)
        kvx[span, 0:128] = block
        kvt[:, span] = block.T

    order = [(e, dz) for dz in (0, 1, 3, 2) for e in (0, 1)]
    for i, at in enumerate(order):
        hand_over(*at)
        if i:
            use(*order[i - 1])
    use(*order[-1])

    for copy in sent + q_sent + k_sent + f_sent:
        copy.wait_send()
    for core in range(2):

        @pl.when(jnp.logical_not(jnp.logical_and(here, c == core)))
        def _():
            kv_copy(0, core).wait_send()

    w_save.wait()


def attend(kvx, kvt, xt, xs, dec, eseg, dkv_out, dq_out, tt, yy, dkv):
    dkv[...] = jnp.zeros_like(dkv)
    seg = eseg[...].astype(F32)

    def one_block(b, _):
        ids = dec[b]
        low, high = jnp.min(ids), jnp.max(ids)
        begin = jnp.sum(jnp.where(seg < low, 1.0, 0.0)).astype(jnp.int32)
        end = jnp.sum(jnp.where(seg <= high, 1.0, 0.0)).astype(jnp.int32)
        j0, j1 = begin // KB, (end + KB - 1) // KB

        def at(j):
            return pl.ds(pl.multiple_of(j * KB, KB), KB)

        def fold(op, v):
            return op(v.reshape(KB // 8, 8, 256), axis=0)

        def scores(j, top):
            both = jnp.dot(kvx[at(j), :], xt[b], preferred_element_type=F32)
            tt[at(j), :] = both
            return jnp.maximum(top, fold(jnp.max, both[:, 0:256]))

        top = lax.fori_loop(j0, j1, scores, jnp.full((8, 256), -3e38, F32))
        top = jnp.max(top, axis=0, keepdims=True)

        def weigh(j, total):
            e = jnp.exp(tt[at(j), 0:256] - top)
            tt[at(j), 0:256] = e
            return total + fold(jnp.sum, e)

        total = lax.fori_loop(j0, j1, weigh, jnp.zeros((8, 256), F32))
        inv = 1.0 / jnp.sum(total, axis=0, keepdims=True)

        def deltas(j, delta):
            low_p = (tt[at(j), 0:256] * inv).astype(BF)
            yy[at(j), 256:512] = low_p
            return delta + fold(jnp.sum, low_p.astype(F32) * tt[at(j), 256:512])

        delta = lax.fori_loop(j0, j1, deltas, jnp.zeros((8, 256), F32))
        delta = jnp.sum(delta, axis=0, keepdims=True)
        inv8 = inv * 0.125

        def grads(j, dq):
            ds = ((tt[at(j), 0:256] * inv8) * (tt[at(j), 256:512] - delta)).astype(BF)
            yy[at(j), 0:256] = ds
            dkv[at(j), :] += jnp.dot(yy[at(j), :], xs[b], preferred_element_type=F32)
            return dq + jnp.dot(kvt[0:64, at(j)], ds, preferred_element_type=F32)

        dq = lax.fori_loop(j0, j1, grads, jnp.zeros((64, 256), F32))
        dq_out[b] = jnp.concatenate([dq[:, 0:128], dq[:, 128:256]], axis=0).T.astype(BF)
        return 0

    lax.fori_loop(0, 8, one_block, 0)
    dkv_out[...] = dkv[...].astype(BF).reshape(dkv_out.shape)


def back(
    dkvp, dqp, enc, w,
    enc_out, q_out, w_out,
    encv, wv, po, pb, ps, rb, gt, gs, qg, cs, cr, ms, mr, keep, fin, fsib, ycs, ycr, yms, ymr,
    loc, sib_s, sib_r, dsend, drecv, qsend, qrecv, csend, crecv, msend, mrecv, ysend, yrecv,
):
    x, xh, z, c, y = coords()
    sibling = dev(x, z, 1 - c, y)
    peers = plane_peers(x, z, c, y) + [dev(x, z, c, mod4(y + 1)), dev(x, z, c, mod4(y + 3))]
    greet(peers)
    p_loc = pltpu.make_async_copy(dkvp.at[pl.ds(c * 4, 4)], po, loc.at[0])
    p_loc.start()
    e_loc = pltpu.make_async_copy(enc, encv.at[c], loc.at[1])
    e_loc.start()
    w_loc = pltpu.make_async_copy(w, wv.at[c], loc.at[2])
    w_loc.start()
    q_loc = pltpu.make_async_copy(dqp.at[xh * 4 + z], qg.at[xh * 4 + z], loc.at[3])
    q_loc.start()
    greeted(peers)

    here = c == xh
    p_sib = remote(dkvp.at[pl.ds((1 - c) * 4, 4)], pb, sib_s.at[0], sib_r.at[0], sibling)
    p_sib.start()
    e_sib = remote(enc, encv.at[c], sib_s.at[1], sib_r.at[1], sibling)
    e_sib.start()
    w_sib = remote(w, wv.at[c], sib_s.at[2], sib_r.at[2], sibling)
    w_sib.start()

    def d_copy(dz):
        tz = mod4(z + dz)
        return remote(ps.at[tz], rb.at[z], dsend.at[dz], drecv.at[dz], dev(c * 2 + x % 2, tz, xh, y))

    p_loc.wait()
    p_sib.wait()
    for dz in (2, 1, 3, 0):
        tz = mod4(z + dz)
        ps[tz] = (po[tz].astype(F32) + pb[tz].astype(F32)).astype(BF)
        if dz:
            d_copy(dz).start()
    d_loc = pltpu.make_async_copy(ps.at[z], rb.at[z], loc.at[4])

    @pl.when(here)
    def _():
        d_loc.start()

    @pl.when(jnp.logical_not(here))
    def _():
        d_copy(0).start()

    q_sent = []
    for dxh in (1, 0):
        for dz in (2, 1, 3, 0):
            if dxh or dz:
                tx, tz = (xh + dxh) % 2, mod4(z + dz)
                copy = remote(
                    dqp.at[tx * 4 + tz], qg.at[xh * 4 + z], qsend.at[dxh, dz], qrecv.at[dxh, dz],
                    dev(tx * 2 + x % 2, tz, c, y),
                )
                copy.start()
                q_sent.append(copy)

    for dz in (0, 1, 3, 2):
        j = mod4(z - dz)
        if dz == 0:

            @pl.when(here)
            def _():
                d_loc.wait()

            @pl.when(jnp.logical_not(here))
            def _():
                arrived(rb.at[j], drecv.at[0])
        else:
            arrived(rb.at[j], drecv.at[dz])
        turned = rb[j].T
        keys = pl.ds(pl.multiple_of(j * 64, 64), 64)
        gt[0, keys, :] = turned[0:64]
        gt[1, keys, :] = turned[64:128]

    own_tok = pl.ds(pl.multiple_of(c * 256, 256), 256)
    sib_tok = pl.ds(pl.multiple_of((1 - c) * 256, 256), 256)
    g_sib = remote(gt.at[:, :, sib_tok], gs.at[c], sib_s.at[3], sib_r.at[3], sibling)
    g_sib.start()
    gs_own = pltpu.make_async_copy(gt.at[:, :, own_tok], gs.at[c], loc.at[5])
    gs_own.start()
    e_loc.wait()
    e_sib.wait()

    def product(a, first, second):
        bx, bz = (second, first) if a == 0 else (first, second)
        columns = pl.ds(pl.multiple_of((row_group(mod4(x + bx)) * 4 + mod4(z + bz)) * 256, 256), 256)
        return jnp.dot(gt[a, :, 0:256], encv[0, :, columns], preferred_element_type=F32) + jnp.dot(
            gt[a, :, 256:512], encv[1, :, columns], preferred_element_type=F32
        )

    sent = []

    def neighbour(a, ring, step):
        along_x = (a == 1) == (ring == 0)
        return dev(mod4(x + step), z, c, y) if along_x else dev(x, mod4(z + step), c, y)

    def send_far(a, slot, ring, value):
        for half in range(2):
            cs[a, slot, half] = value[half * 128 : half * 128 + 128].astype(BF)
            at = (a, slot, half)
            copy = remote(cs.at[at], cr.at[at], csend.at[at], crecv.at[at], neighbour(a, ring, 1 - 2 * half))
            copy.start()
            sent.append(copy)

    def send_near(a, slot, ring, values):
        for half in range(2):
            value = values[half]()
            at = (a, slot, half)
            arrived(cr.at[at], crecv.at[at])
            keep_half = pl.ds(half * 128, 128)
            rest = slice(128, 256) if half == 0 else slice(0, 128)
            this = slice(0, 128) if half == 0 else slice(128, 256)
            ms[a, slot, half, pl.ds((1 - half) * 128, 128), :] = value[rest].astype(BF)
            ms[a, slot, half, keep_half, :] = (value[this] + cr[a, slot, half].astype(F32)).astype(BF)
            copy = remote(ms.at[at], mr.at[at], msend.at[at], mrecv.at[at], neighbour(a, ring, 1 - 2 * half))
            copy.start()
            sent.append(copy)

    def collect(a, slot, value):
        for half in range(2):
            at = (a, slot, half)
            arrived(mr.at[at], mrecv.at[at])
            value = value + mr[a, slot, half].astype(F32)
        return value

    def far(slot):
        for a in range(2):
            send_far(a, slot, 0, product(a, 2, slot))

    def near(slot):
        for a in range(2):
            send_near(a, slot, 0, [lambda a=a: product(a, 1, slot), lambda a=a: product(a, 3, slot)])

    def ahead(slot):
        for a in range(2):
            keep[a, slot] = product(a, 0, slot)

    def enc_rows(dy, r):
        group = mod4(y + dy)
        total = None
        for half in range(2):
            for a in range(2):
                term = jnp.dot(wv[half, a, group, r], gs[half, a], preferred_element_type=F32)
                total = term if total is None else total + term
        return total

    def y_send(src, dst, i, step):
        copy = remote(src, dst, ysend.at[i], yrecv.at[i], dev(x, z, c, mod4(y + step)))
        copy.start()
        sent.append(copy)

    def y_far():
        for half in range(2):
            for r in range(2):
                ycs[half, r] = enc_rows(2, 2 * half + r).astype(BF)
            y_send(ycs.at[half], ycr.at[half], half, 1 - 2 * half)

    def y_free():
        for half in range(2):
            for r in range(2):
                yms[half, 1 - half, r] = enc_rows(1 + 2 * half, 2 * (1 - half) + r).astype(BF)
            y_send(yms.at[half, 1 - half], ymr.at[half, 1 - half], 2 + half, 1 - 2 * half)

    def y_near():
        for half in range(2):
            for r in range(2):
                value = enc_rows(1 + 2 * half, 2 * half + r)
                if r == 0:
                    arrived(ycr.at[half], yrecv.at[half])
                yms[half, half, r] = (value + ycr[half, r].astype(F32)).astype(BF)
            y_send(yms.at[half, half], ymr.at[half, half], 4 + half, 1 - 2 * half)

    far(2)
    gs_own.wait()
    g_sib.wait()
    w_loc.wait()
    w_sib.wait()
    y_far()
    far(1)
    near(2)
    y_free()
    far(3)
    near(1)
    ahead(2)
    far(0)
    near(3)
    y_near()
    for a in range(2):
        send_far(a, 4, 1, collect(a, 2, keep[a, 2]))
    near(0)
    ahead(1)
    ahead(3)
    ahead(0)

    q_loc.wait()
    for dxh in range(2):
        for dz in range(4):
            if dxh or dz:
                src = ((xh + dxh) % 2) * 4 + mod4(z - dz)
                arrived(qg.at[src], qrecv.at[dxh, dz])
    q_out[...] = qg[...]

    for a in range(2):
        for slot in (1, 3):
            keep[a, slot] = collect(a, slot, keep[a, slot])
    for a in range(2):
        send_near(a, 4, 1, [lambda a=a: keep[a, 1], lambda a=a: keep[a, 3]])

    for r in range(4):
        total = enc_rows(0, r).astype(BF).astype(F32)
        for half in range(2):
            if r == 0:
                arrived(ymr.at[half, 1 - half], yrecv.at[2 + half])
                arrived(ymr.at[half, half], yrecv.at[4 + half])
            total = total + ymr[half, r // 2, r % 2].astype(F32)
        enc_out[pl.ds(r * 256, 256), :] = total.astype(BF)

    for a in range(2):
        fin[a] = collect(a, 4, collect(a, 0, keep[a, 0]))
    mine = pl.ds(pl.multiple_of(c * 128, 128), 128)
    theirs = pl.ds(pl.multiple_of((1 - c) * 128, 128), 128)
    f_sib = remote(fin.at[:, :, theirs], fsib, sib_s.at[4], sib_r.at[4], sibling)
    f_sib.start()
    w_out[:, pl.ds(pl.multiple_of(c * 256, 256), 256), :] = fin[:, :, mine]
    for copy in q_sent + sent + [d_copy(dz) for dz in (1, 2, 3)]:
        copy.wait_send()

    @pl.when(jnp.logical_not(here))
    def _():
        d_copy(0).wait_send()

    f_sib.wait()
    w_out[:, pl.ds(pl.multiple_of((1 - c) * 256, 256), 256), :] = fsib[...]


def finish(enc_t, qg, w_t, enc_out, q_out, w_out):
    enc_out[...] = enc_t[...].T
    for i in range(4):
        tile = pl.ds(i * 128, 128)
        even, odd = qg[2 * i].astype(F32), qg[2 * i + 1].astype(F32)
        q_out[0:128, tile] = halves(even, odd, False, True).astype(BF)
        q_out[128:256, tile] = halves(even, odd, True, False).astype(BF)
    for a in range(2):
        w_out[a] = w_t[a].T


VM = pl.BlockSpec(memory_space=pltpu.VMEM)
ANY = pl.BlockSpec(memory_space=pl.ANY)
DMA = pltpu.SemaphoreType.DMA


def params(collective_id=None):
    if collective_id is None:
        return pltpu.CompilerParams(vmem_limit_bytes=60 << 20)
    return pltpu.CompilerParams(
        collective_id=collective_id, has_side_effects=True, vmem_limit_bytes=60 << 20
    )


def body(enc_out, dec_query, ctx_grad, kv_weight, enc_seg, dec_seg):
    enc = enc_out[0]
    eseg = enc_seg.reshape(32, 128)
    dseg = dec_seg.reshape(2, 128)
    shape = jax.ShapeDtypeStruct
    wg, kvx, kvt, xt, xs, dec = pl.pallas_call(
        front,
        out_shape=(
            shape((2, 4, 4, 256, 256), BF),
            shape((4096, 256), BF),
            shape((128, 4096), BF),
            shape((8, 256, 512), BF),
            shape((8, 512, 128), BF),
            shape((8, 8, 256), F32),
        ),
        in_specs=[ANY, VM, VM, ANY, VM, VM],
        out_specs=(ANY, VM, VM, VM, VM, VM),
        scratch_shapes=[
            pltpu.VMEM((2, 256, 4096), BF),
            pltpu.VMEM((2, 4, 4, 256, 256), BF),
            pltpu.VMEM((2, 512, 256), F32),
            pltpu.VMEM((4, 512, 128), BF),
            pltpu.VMEM((8, 512, 128), BF),
            pltpu.VMEM((8, 272, 128), BF),
            pltpu.VMEM((8, 272, 128), BF),
            DMA((5,)), DMA((2,)), DMA((2,)),
            DMA((2, 4, 4, 2)), DMA((2, 4, 4, 2)),
            DMA((2, 4)), DMA((2, 4)),
            DMA((4, 2)), DMA((2, 4)),
            DMA((2, 4)), DMA((2, 4)),
        ],
        compiler_params=params(1),
        name="front",
    )(enc, dec_query[0], ctx_grad[0], kv_weight, dseg, eseg)

    dkvp, dqp = pl.pallas_call(
        attend,
        out_shape=(shape((8, 512, 128), BF), shape((8, 128, 128), BF)),
        in_specs=[VM] * 6,
        out_specs=(VM, VM),
        scratch_shapes=[
            pltpu.VMEM((4096, 512), F32),
            pltpu.VMEM((4096, 512), BF),
            pltpu.VMEM((4096, 128), F32),
        ],
        compiler_params=params(),
        name="attend",
    )(kvx, kvt, xt, xs, dec, eseg)

    enc_t, qg, w_t = pl.pallas_call(
        back,
        out_shape=(shape((1024, 256), BF), shape((8, 128, 128), BF), shape((2, 512, 128), F32)),
        in_specs=[ANY, ANY, ANY, ANY],
        out_specs=(VM, VM, VM),
        scratch_shapes=[
            pltpu.VMEM((2, 256, 4096), BF),
            pltpu.VMEM((2, 2, 4, 4, 256, 256), BF),
            pltpu.VMEM((4, 512, 128), BF),
            pltpu.VMEM((4, 512, 128), BF),
            pltpu.VMEM((4, 512, 128), BF),
            pltpu.VMEM((4, 512, 128), BF),
            pltpu.VMEM((2, 256, 512), BF),
            pltpu.VMEM((2, 2, 256, 256), BF),
            pltpu.VMEM((8, 128, 128), BF),
            pltpu.VMEM((2, 5, 2, 128, 256), BF),
            pltpu.VMEM((2, 5, 2, 128, 256), BF),
            pltpu.VMEM((2, 5, 2, 256, 256), BF),
            pltpu.VMEM((2, 5, 2, 256, 256), BF),
            pltpu.VMEM((2, 4, 256, 256), F32),
            pltpu.VMEM((2, 256, 256), F32),
            pltpu.VMEM((2, 256, 128), F32),
            pltpu.VMEM((2, 2, 256, 256), BF),
            pltpu.VMEM((2, 2, 256, 256), BF),
            pltpu.VMEM((2, 2, 2, 256, 256), BF),
            pltpu.VMEM((2, 2, 2, 256, 256), BF),
            DMA((6,)), DMA((5,)), DMA((5,)),
            DMA((4,)), DMA((4,)),
            DMA((2, 4)), DMA((2, 4)),
            DMA((2, 5, 2)), DMA((2, 5, 2)),
            DMA((2, 5, 2)), DMA((2, 5, 2)),
            DMA((6,)), DMA((6,)),
        ],
        compiler_params=params(2),
        name="back",
    )(dkvp, dqp, enc, wg)

    enc_grad, q_grad, w_grad = pl.pallas_call(
        finish,
        out_shape=(shape((256, 1024), BF), shape((256, 512), BF), shape((2, 128, 512), F32)),
        in_specs=[VM] * 3,
        out_specs=(VM, VM, VM),
        compiler_params=params(),
        name="finish",
    )(enc_t, qg, w_t)
    return enc_grad[None], q_grad[None], w_grad


def solution(mesh):
    placed = (
        P("dp", "seq", None),
        P("dp", "seq", "mp"),
        P("dp", "seq", "mp"),
        P(None, ("dp", "seq"), "mp"),
        P("dp", None),
        P("dp", "seq"),
    )
    return jax.shard_map(
        body,
        mesh=mesh,
        in_specs=placed,
        out_specs=(P("dp", "seq", "mp"), P("dp", "seq", "mp"), P(None, ("dp", "seq"), "mp")),
        check_vma=False,
    )
```

time: 156 us -> 131 us (0.84)
  Pallas kernels: 149 us -> 130 us
  local copies, waits for them, and re-layouts: 6.11 us -> 0 us
    pallas_call x1, Pallas kernels: 65.8 us -> 56.3 us  [body(): pl.pallas_call(front, out_shape=(shape((2, 4, 4, 256, 256), BF), shape((4...]
    pallas_call x1, Pallas kernels: 30.9 us -> 24.7 us  [body(): pl.pallas_call(attend, out_shape=(shape((8, 512, 128), BF), shape((8, 128...]
    unnamed x5 -> x0, local copies, waits for them, and re-layouts: 4.83 us -> none
    pallas_call x1 -> x2, Pallas kernels: 52.6 us -> 49.5 us  [the longest x1 46.9 us: body(): pl.pallas_call(back, out_shape=(shape((1024, 256), BF), shape((8, 128, 12...]
where the time goes in v2:
time: 131 us
  Pallas kernels  130 us (99%)
    pallas_call x1, Pallas kernels, body(): pl.pallas_call(front, out_shape=(shape((2, 4, 4, 256, 256), BF), shape((4...  56.3 us
    pallas_call x1, Pallas kernels, body(): pl.pallas_call(back, out_shape=(shape((1024, 256), BF), shape((8, 128, 12...  46.9 us
    pallas_call x1, Pallas kernels, body(): pl.pallas_call(attend, out_shape=(shape((8, 512, 128), BF), shape((8, 128...  24.7 us

profile of v2, /device:TPU:1, one launch (start us, length us, event | category | flops | bytes accessed | tf_op | source)
XLA Modules:
  0.0 131.1 jit_solution(13435176785218553009)
XLA Ops:
  0.6 56.3 %front.1 = (bf16[2,4,4,256,256]{4,3,2,1,0:T(8,128)(2,1)}, bf16[4096,256]{1,0:T(8,128)(2,1)}, bf16[128,4096]{1,0:T(8,128)(2,1)}, bf16[8,256,512]{2,1,0:T(8,128)(2...) custom-call(bf16[256,4096]{1,0:T(8,128)(2,1)} %bitcast.7, bf16[256,512]{1,0:T(8,128)(2,1)} %bitcast.9, ...), custom_call_target="tpu_custom_call" | custom-call | tf_op jit(solution)/shard_map/front/pallas_call | solution.py:664
  57.0 24.7 %attend.1 = (bf16[8,512,128]{2,1,0:T(8,128)(2,1)}, bf16[8,128,128]{2,1,0:T(8,128)(2,1)}) custom-call(bf16[4096,256]{1,0:T(8,128)(2,1)} %get-tuple-element.17.kvx, bf16[128,4096]{1,0:T(8,128)(2,1)} %get-tuple-element.18.kvt, bf16[8,256,512]{2,1,0:T(8,128)(2,1)} %get-tuple-element.19.xt, bf16[8,512,128]{2,1,0:T(8,128)(2,1)} %get-tuple-element.20.xs, ...), custom_call_target="tpu_custom_call" | custom-call | tf_op jit(solution)/shard_map/attend/pallas_call | solution.py:694
  81.7 46.9 %back.1 = (bf16[1024,256]{1,0:T(8,128)(2,1)}, bf16[8,128,128]{2,1,0:T(8,128)(2,1)}, f32[2,512,128]{2,1,0:T(8,128)}) custom-call(bf16[8,512,128]{2,1,0:T(8,128)(2,1)} %get-tuple-element.22.dkvp, bf16[8,128,128]{2,1,0:T(8,128)(2,1)} %get-tuple-element.23.dqp, bf16[256,4096]{1,0:T(8,128)(2,1)} %bitcast.8, bf16[2,4,4,256,256]{4,3,2,1,0:T(8,128)(2,1)} %get-tuple-element.24.w), custom_call_target="tpu_custom_call" | custom-call | tf_op jit(solution)/shard_map/back/pallas_call | solution.py:708
  128.5 2.6 %finish.1 = (bf16[256,1024]{1,0:T(8,128)(2,1)}, bf16[256,512]{1,0:T(8,128)(2,1)}, f32[2,128,512]{2,1,0:T(8,128)}) custom-call(bf16[1024,256]{1,0:T(8,128)(2,1)} %get-tuple-element.25.enc_t, bf16[8,128,128]{2,1,0:T(8,128)(2,1)} %get-tuple-element.26.qg, f32[2,512,128]{2,1,0:T(8,128)} %get-tuple-element.27.w_t), custom_call_target="tpu_custom_call" | custom-call | tf_op jit(solution)/shard_map/finish/pallas_call | solution.py:745

commit v3 on v2

--- a/solution.py
+++ b/solution.py
@@ -11,7 +11,7 @@
 BF = jnp.bfloat16
 F32 = jnp.float32
 NEG = -1e30
-KB = 512
+KB = 256
 
 
 def coords():
@@ -72,9 +72,9 @@
 
 def front(
     enc, q, do, w, dseg, eseg,
-    wg_out, kvx, kvt, xt, xs, dec_out,
-    encv, wg, acc, kvs, kvb, qs, qb,
-    loc, sib_s, sib_r, ws, wr, qsend, qrecv, ksend, krecv, fsend, frecv,
+    wg_out, kvx_out, kvt_out, xt_out, xs_out, spans,
+    encv, wg, acc, kvs, kvb, qs, qb, kvx, kvt, xt, xs,
+    loc, save, sib_s, sib_r, ws, wr, qsend, qrecv, ksend, krecv, fsend, frecv,
 ):
     x, xh, z, c, y = coords()
     me = row_group(x)
@@ -226,7 +226,14 @@
         row = lax.broadcasted_iota(jnp.int32, (16, 256), 0)
         differs = (row < 4) & (row.astype(F32) != ids)
         xt[b, 128:144, 0:256] = jnp.where(differs, NEG, 0.0).astype(BF)
-        dec_out[b] = jnp.broadcast_to(ids, (8, 256))
+        seg = eseg[...].astype(F32)
+        low_id, high_id = jnp.min(ids, axis=1, keepdims=True), jnp.max(ids, axis=1, keepdims=True)
+        begin = jnp.sum(jnp.where(seg < low_id, 1.0, 0.0), axis=(0, 1), keepdims=True)
+        end = jnp.sum(jnp.where(seg <= high_id, 1.0, 0.0), axis=(0, 1), keepdims=True)
+        begin = jnp.floor(begin * (1.0 / 128)) * 128.0
+        count = jnp.floor((end - begin + (KB - 1)) * (1.0 / KB))
+        begin = jnp.minimum(begin, 4096.0 - count * KB)
+        spans[pl.ds(b, 1), :] = jnp.where(lanes_of((1, 128)) == 0, begin, count).astype(jnp.int32)
         return 0
 
     for first in (1, 3, 2):
@@ -239,6 +246,12 @@
             multiply(a, first, 3)
         if first != 2:
             lax.fori_loop(0 if first == 1 else 4, 4 if first == 1 else 8, prepare, 0)
+    saved = [
+        pltpu.make_async_copy(xt, xt_out, save.at[8]),
+        pltpu.make_async_copy(xs, xs_out, save.at[9]),
+    ]
+    for copy in saved:
+        copy.start()
     for first in (0, 1, 3, 2):
         for a in range(2):
             take(a, first, 2)
@@ -317,6 +330,12 @@
         span = pl.ds(pl.multiple_of(src * 512, 512), 512)
         kvx[span, 0:128] = block
         kvt[:, span] = block.T
+        for copy in (
+            pltpu.make_async_copy(kvx.at[span], kvx_out.at[span], save.at[e * 4 + dz]),
+            pltpu.make_async_copy(kvt.at[:, span], kvt_out.at[:, span], save.at[10 + e * 4 + dz]),
+        ):
+            copy.start()
+            saved.append(copy)
 
     order = [(e, dz) for dz in (0, 1, 3, 2) for e in (0, 1)]
     for i, at in enumerate(order):
@@ -334,57 +353,88 @@
             kv_copy(0, core).wait_send()
 
     w_save.wait()
-
-
-def attend(kvx, kvt, xt, xs, dec, eseg, dkv_out, dq_out, tt, yy, dkv):
+    for copy in saved:
+        copy.wait()
+
+
+def attend(
+    spans, kvx_in, kvt_in, xt_in, xs_in, dkv_out, dq_out, kvx, kvt, xt, xs, tt, yy, dkv, sem, xt_sem, xs_sem
+):
+    kvx_copy = pltpu.make_async_copy(kvx_in, kvx, sem.at[0])
+    kvt_copy = pltpu.make_async_copy(kvt_in, kvt, sem.at[1])
+
+    def xt_copy(b):
+        return pltpu.make_async_copy(xt_in.at[b], xt.at[b], xt_sem.at[b])
+
+    def xs_copy(b):
+        return pltpu.make_async_copy(xs_in.at[b], xs.at[b], xs_sem.at[b])
+
+    xt_copy(0).start()
+    kvx_copy.start()
+    xs_copy(0).start()
+    kvt_copy.start()
+    for b in range(1, 8):
+        xt_copy(b).start()
+        xs_copy(b).start()
     dkv[...] = jnp.zeros_like(dkv)
-    seg = eseg[...].astype(F32)
+    kvx_copy.wait()
 
     def one_block(b, _):
-        ids = dec[b]
-        low, high = jnp.min(ids), jnp.max(ids)
-        begin = jnp.sum(jnp.where(seg < low, 1.0, 0.0)).astype(jnp.int32)
-        end = jnp.sum(jnp.where(seg <= high, 1.0, 0.0)).astype(jnp.int32)
-        j0, j1 = begin // KB, (end + KB - 1) // KB
-
-        def at(j):
-            return pl.ds(pl.multiple_of(j * KB, KB), KB)
+        begin, count = spans[b, 0], spans[b, 1]
+        xt_copy(b).wait()
+
+        def sweep(step, carry):
+            done = 0
+            for blocks in (3, 2, 1):
+                times = (count - done) // blocks
+
+                def piece(i, value, done=done, blocks=blocks):
+                    first = pl.multiple_of(begin + (done + i * blocks) * KB, 128)
+                    return step(pl.ds(first, blocks * KB), value)
+
+                carry = lax.fori_loop(0, times, piece, carry)
+                done = done + times * blocks
+            return carry
 
         def fold(op, v):
-            return op(v.reshape(KB // 8, 8, 256), axis=0)
-
-        def scores(j, top):
-            both = jnp.dot(kvx[at(j), :], xt[b], preferred_element_type=F32)
-            tt[at(j), :] = both
+            return op(v.reshape(v.shape[0] // 8, 8, 256), axis=0)
+
+        def scores(rows, top):
+            both = jnp.dot(kvx[rows, :], xt[b], preferred_element_type=F32)
+            tt[rows, :] = both
             return jnp.maximum(top, fold(jnp.max, both[:, 0:256]))
 
-        top = lax.fori_loop(j0, j1, scores, jnp.full((8, 256), -3e38, F32))
+        top = sweep(scores, jnp.full((8, 256), -3e38, F32))
         top = jnp.max(top, axis=0, keepdims=True)
 
-        def weigh(j, total):
-            e = jnp.exp(tt[at(j), 0:256] - top)
-            tt[at(j), 0:256] = e
+        def weigh(rows, total):
+            e = jnp.exp(tt[rows, 0:256] - top)
+            tt[rows, 0:256] = e
             return total + fold(jnp.sum, e)
 
-        total = lax.fori_loop(j0, j1, weigh, jnp.zeros((8, 256), F32))
+        total = sweep(weigh, jnp.zeros((8, 256), F32))
         inv = 1.0 / jnp.sum(total, axis=0, keepdims=True)
 
-        def deltas(j, delta):
-            low_p = (tt[at(j), 0:256] * inv).astype(BF)
-            yy[at(j), 256:512] = low_p
-            return delta + fold(jnp.sum, low_p.astype(F32) * tt[at(j), 256:512])
-
-        delta = lax.fori_loop(j0, j1, deltas, jnp.zeros((8, 256), F32))
+        def deltas(rows, delta):
+            low_p = (tt[rows, 0:256] * inv).astype(BF)
+            yy[rows, 256:512] = low_p
+            return delta + fold(jnp.sum, low_p.astype(F32) * tt[rows, 256:512])
+
+        delta = sweep(deltas, jnp.zeros((8, 256), F32))
         delta = jnp.sum(delta, axis=0, keepdims=True)
         inv8 = inv * 0.125
-
-        def grads(j, dq):
-            ds = ((tt[at(j), 0:256] * inv8) * (tt[at(j), 256:512] - delta)).astype(BF)
-            yy[at(j), 0:256] = ds
-            dkv[at(j), :] += jnp.dot(yy[at(j), :], xs[b], preferred_element_type=F32)
-            return dq + jnp.dot(kvt[0:64, at(j)], ds, preferred_element_type=F32)
-
-        dq = lax.fori_loop(j0, j1, grads, jnp.zeros((64, 256), F32))
+        xs_copy(b).wait()
+
+        @pl.when(b == 0)
+        def _():
+            kvt_copy.wait()
+
+        def grads(rows, dq):
+            yy[rows, 0:256] = ((tt[rows, 0:256] * inv8) * (tt[rows, 256:512] - delta)).astype(BF)
+            dkv[rows, :] += jnp.dot(yy[rows, :], xs[b], preferred_element_type=F32)
+            return dq + jnp.dot(kvt[0:64, rows], yy[rows, 0:256], preferred_element_type=F32)
+
+        dq = sweep(grads, jnp.zeros((64, 256), F32))
         dq_out[b] = jnp.concatenate([dq[:, 0:128], dq[:, 128:256]], axis=0).T.astype(BF)
         return 0
 
@@ -661,7 +711,7 @@
     eseg = enc_seg.reshape(32, 128)
     dseg = dec_seg.reshape(2, 128)
     shape = jax.ShapeDtypeStruct
-    wg, kvx, kvt, xt, xs, dec = pl.pallas_call(
+    wg, kvx, kvt, xt, xs, spans = pl.pallas_call(
         front,
         out_shape=(
             shape((2, 4, 4, 256, 256), BF),
@@ -669,10 +719,10 @@
             shape((128, 4096), BF),
             shape((8, 256, 512), BF),
             shape((8, 512, 128), BF),
-            shape((8, 8, 256), F32),
+            shape((8, 128), jnp.int32),
         ),
         in_specs=[ANY, VM, VM, ANY, VM, VM],
-        out_specs=(ANY, VM, VM, VM, VM, VM),
+        out_specs=(ANY, ANY, ANY, ANY, ANY, VM),
         scratch_shapes=[
             pltpu.VMEM((2, 256, 4096), BF),
             pltpu.VMEM((2, 4, 4, 256, 256), BF),
@@ -681,7 +731,11 @@
             pltpu.VMEM((8, 512, 128), BF),
             pltpu.VMEM((8, 272, 128), BF),
             pltpu.VMEM((8, 272, 128), BF),
-            DMA((5,)), DMA((2,)), DMA((2,)),
+            pltpu.VMEM((4096, 256), BF),
+            pltpu.VMEM((128, 4096), BF),
+            pltpu.VMEM((8, 256, 512), BF),
+            pltpu.VMEM((8, 512, 128), BF),
+            DMA((5,)), DMA((18,)), DMA((2,)), DMA((2,)),
             DMA((2, 4, 4, 2)), DMA((2, 4, 4, 2)),
             DMA((2, 4)), DMA((2, 4)),
             DMA((4, 2)), DMA((2, 4)),
@@ -694,16 +748,21 @@
     dkvp, dqp = pl.pallas_call(
         attend,
         out_shape=(shape((8, 512, 128), BF), shape((8, 128, 128), BF)),
-        in_specs=[VM] * 6,
+        in_specs=[pl.BlockSpec(memory_space=pltpu.SMEM), ANY, ANY, ANY, ANY],
         out_specs=(VM, VM),
         scratch_shapes=[
+            pltpu.VMEM((4096, 256), BF),
+            pltpu.VMEM((128, 4096), BF),
+            pltpu.VMEM((8, 256, 512), BF),
+            pltpu.VMEM((8, 512, 128), BF),
             pltpu.VMEM((4096, 512), F32),
             pltpu.VMEM((4096, 512), BF),
             pltpu.VMEM((4096, 128), F32),
+            DMA((2,)), DMA((8,)), DMA((8,)),
         ],
         compiler_params=params(),
         name="attend",
-    )(kvx, kvt, xt, xs, dec, eseg)
+    )(spans, kvx, kvt, xt, xs)
 
     enc_t, qg, w_t = pl.pallas_call(
         back,

time: 131 us -> 130 us (level)
    pallas_call x1, Pallas kernels: 56.3 us -> 55 us  [body(): pl.pallas_call(front, out_shape=(shape((2, 4, 4, 256, 256), BF), shape((4...]
where the time goes in v3:
time: 130 us
  Pallas kernels  129 us (99%)
    pallas_call x1, Pallas kernels, body(): pl.pallas_call(front, out_shape=(shape((2, 4, 4, 256, 256), BF), shape((4...  55 us
    pallas_call x1, Pallas kernels, body(): pl.pallas_call(back, out_shape=(shape((1024, 256), BF), shape((8, 128, 12...  47.9 us
    pallas_call x1, Pallas kernels, body(): pl.pallas_call(attend, out_shape=(shape((8, 512, 128), BF), shape((8, 128...  23.9 us
    pallas_call x1, Pallas kernels, body(): pl.pallas_call(finish, out_shape=(shape((256, 1024), BF), shape((256, 512...  2.61 us

profile of v3, /device:TPU:1, one launch (start us, length us, event | category | flops | bytes accessed | tf_op | source)
XLA Modules:
  0.0 130.0 jit_solution(2379617584425731409)
XLA Ops:
  0.6 55.0 %front.1 = (bf16[2,4,4,256,256]{4,3,2,1,0:T(8,128)(2,1)}, bf16[4096,256]{1,0:T(8,128)(2,1)}, bf16[128,4096]{1,0:T(8,128)(2,1)}, bf16[8,256,512]{2,1,0:T(8,128)(2...) custom-call(bf16[256,4096]{1,0:T(8,128)(2,1)} %bitcast.7, bf16[256,512]{1,0:T(8,128)(2,1)} %bitcast.9, ...), custom_call_target="tpu_custom_call" | custom-call | tf_op jit(solution)/shard_map/front/pallas_call | solution.py:714
  55.6 23.9 %attend.1 = (bf16[8,512,128]{2,1,0:T(8,128)(2,1)}, bf16[8,128,128]{2,1,0:T(8,128)(2,1)}) custom-call(s32[8,128]{1,0:T(8,128)} %get-tuple-element.17.spans, bf16[4096,256]{1,0:T(8,128)(2,1)} %get-tuple-element.18.kvx_in, bf16[128,4096]{1,0:T(8,128)(2,1)} %get-tuple-element.19.kvt_in, bf16[8,256,512]{2,1,0:T(8,128)(2,1)} %get-tuple-element.20.xt_in, ...), custom_call_target="tpu_custom_call" | custom-call | tf_op jit(solution)/shard_map/attend/pallas_call | solution.py:748
  79.5 47.9 %back.1 = (bf16[1024,256]{1,0:T(8,128)(2,1)}, bf16[8,128,128]{2,1,0:T(8,128)(2,1)}, f32[2,512,128]{2,1,0:T(8,128)}) custom-call(bf16[8,512,128]{2,1,0:T(8,128)(2,1)} %get-tuple-element.22.dkvp, bf16[8,128,128]{2,1,0:T(8,128)(2,1)} %get-tuple-element.23.dqp, bf16[256,4096]{1,0:T(8,128)(2,1)} %bitcast.8, bf16[2,4,4,256,256]{4,3,2,1,0:T(8,128)(2,1)} %get-tuple-element.24.w), custom_call_target="tpu_custom_call" | custom-call | tf_op jit(solution)/shard_map/back/pallas_call | solution.py:767
  127.4 2.6 %finish.1 = (bf16[256,1024]{1,0:T(8,128)(2,1)}, bf16[256,512]{1,0:T(8,128)(2,1)}, f32[2,128,512]{2,1,0:T(8,128)}) custom-call(bf16[1024,256]{1,0:T(8,128)(2,1)} %get-tuple-element.25.enc_t, bf16[8,128,128]{2,1,0:T(8,128)(2,1)} %get-tuple-element.26.qg, f32[2,512,128]{2,1,0:T(8,128)} %get-tuple-element.27.w_t), custom_call_target="tpu_custom_call" | custom-call | tf_op jit(solution)/shard_map/finish/pallas_call | solution.py:804

commit v4 on v3

--- a/solution.py
+++ b/solution.py
@@ -358,7 +358,7 @@
 
 
 def attend(
-    spans, kvx_in, kvt_in, xt_in, xs_in, dkv_out, dq_out, kvx, kvt, xt, xs, tt, yy, dkv, sem, xt_sem, xs_sem
+    spans, kvx_in, kvt_in, xt_in, xs_in, dkv_out, dq_out, kvx, kvt, xt, xs, tt, low_ps, dkv, sem, xt_sem, xs_sem
 ):
     kvx_copy = pltpu.make_async_copy(kvx_in, kvx, sem.at[0])
     kvt_copy = pltpu.make_async_copy(kvt_in, kvt, sem.at[1])
@@ -385,12 +385,12 @@
 
         def sweep(step, carry):
             done = 0
-            for blocks in (3, 2, 1):
+            for blocks in (8, 3, 2, 1):
                 times = (count - done) // blocks
 
                 def piece(i, value, done=done, blocks=blocks):
                     first = pl.multiple_of(begin + (done + i * blocks) * KB, 128)
-                    return step(pl.ds(first, blocks * KB), value)
+                    return step(first, blocks * KB, value)
 
                 carry = lax.fori_loop(0, times, piece, carry)
                 done = done + times * blocks
@@ -399,7 +399,8 @@
         def fold(op, v):
             return op(v.reshape(v.shape[0] // 8, 8, 256), axis=0)
 
-        def scores(rows, top):
+        def scores(first, length, top):
+            rows = pl.ds(first, length)
             both = jnp.dot(kvx[rows, :], xt[b], preferred_element_type=F32)
             tt[rows, :] = both
             return jnp.maximum(top, fold(jnp.max, both[:, 0:256]))
@@ -407,7 +408,8 @@
         top = sweep(scores, jnp.full((8, 256), -3e38, F32))
         top = jnp.max(top, axis=0, keepdims=True)
 
-        def weigh(rows, total):
+        def weigh(first, length, total):
+            rows = pl.ds(first, length)
             e = jnp.exp(tt[rows, 0:256] - top)
             tt[rows, 0:256] = e
             return total + fold(jnp.sum, e)
@@ -415,9 +417,10 @@
         total = sweep(weigh, jnp.zeros((8, 256), F32))
         inv = 1.0 / jnp.sum(total, axis=0, keepdims=True)
 
-        def deltas(rows, delta):
+        def deltas(first, length, delta):
+            rows = pl.ds(first, length)
             low_p = (tt[rows, 0:256] * inv).astype(BF)
-            yy[rows, 256:512] = low_p
+            low_ps[rows, :] = low_p
             return delta + fold(jnp.sum, low_p.astype(F32) * tt[rows, 256:512])
 
         delta = sweep(deltas, jnp.zeros((8, 256), F32))
@@ -429,10 +432,15 @@
         def _():
             kvt_copy.wait()
 
-        def grads(rows, dq):
-            yy[rows, 0:256] = ((tt[rows, 0:256] * inv8) * (tt[rows, 256:512] - delta)).astype(BF)
-            dkv[rows, :] += jnp.dot(yy[rows, :], xs[b], preferred_element_type=F32)
-            return dq + jnp.dot(kvt[0:64, rows], yy[rows, 0:256], preferred_element_type=F32)
+        def grads(first, length, dq):
+            for part in range(0, length, KB):
+                rows = pl.ds(pl.multiple_of(first + part, 128), KB)
+                ds = ((tt[rows, 0:256] * inv8) * (tt[rows, 256:512] - delta)).astype(BF)
+                dkv[rows, :] += jnp.dot(ds, xs[b, 0:256], preferred_element_type=F32) + jnp.dot(
+                    low_ps[rows, :], xs[b, 256:512], preferred_element_type=F32
+                )
+                dq = dq + jnp.dot(kvt[0:64, rows], ds, preferred_element_type=F32)
+            return dq
 
         dq = sweep(grads, jnp.zeros((64, 256), F32))
         dq_out[b] = jnp.concatenate([dq[:, 0:128], dq[:, 128:256]], axis=0).T.astype(BF)
@@ -647,7 +655,11 @@
             if dxh or dz:
                 src = ((xh + dxh) % 2) * 4 + mod4(z - dz)
                 arrived(qg.at[src], qrecv.at[dxh, dz])
-    q_out[...] = qg[...]
+    for i in range(4):
+        tile = pl.ds(i * 128, 128)
+        even, odd = qg[2 * i].astype(F32), qg[2 * i + 1].astype(F32)
+        q_out[0:128, tile] = halves(even, odd, False, True).astype(BF)
+        q_out[128:256, tile] = halves(even, odd, True, False).astype(BF)
 
     for a in range(2):
         for slot in (1, 3):
@@ -662,15 +674,15 @@
                 arrived(ymr.at[half, 1 - half], yrecv.at[2 + half])
                 arrived(ymr.at[half, half], yrecv.at[4 + half])
             total = total + ymr[half, r // 2, r % 2].astype(F32)
-        enc_out[pl.ds(r * 256, 256), :] = total.astype(BF)
-
-    for a in range(2):
-        fin[a] = collect(a, 4, collect(a, 0, keep[a, 0]))
+        enc_out[:, pl.ds(r * 256, 256)] = total.T.astype(BF)
+
+    for a in range(2):
+        fin[a] = collect(a, 4, collect(a, 0, keep[a, 0])).T
     mine = pl.ds(pl.multiple_of(c * 128, 128), 128)
     theirs = pl.ds(pl.multiple_of((1 - c) * 128, 128), 128)
-    f_sib = remote(fin.at[:, :, theirs], fsib, sib_s.at[4], sib_r.at[4], sibling)
+    f_sib = remote(fin.at[:, theirs], fsib, sib_s.at[4], sib_r.at[4], sibling)
     f_sib.start()
-    w_out[:, pl.ds(pl.multiple_of(c * 256, 256), 256), :] = fin[:, :, mine]
+    w_out[:, :, pl.ds(pl.multiple_of(c * 256, 256), 256)] = fin[:, mine]
     for copy in q_sent + sent + [d_copy(dz) for dz in (1, 2, 3)]:
         copy.wait_send()
 
@@ -679,18 +691,29 @@
         d_copy(0).wait_send()
 
     f_sib.wait()
-    w_out[:, pl.ds(pl.multiple_of((1 - c) * 256, 256), 256), :] = fsib[...]
-
-
-def finish(enc_t, qg, w_t, enc_out, q_out, w_out):
-    enc_out[...] = enc_t[...].T
-    for i in range(4):
-        tile = pl.ds(i * 128, 128)
-        even, odd = qg[2 * i].astype(F32), qg[2 * i + 1].astype(F32)
-        q_out[0:128, tile] = halves(even, odd, False, True).astype(BF)
-        q_out[128:256, tile] = halves(even, odd, True, False).astype(BF)
-    for a in range(2):
-        w_out[a] = w_t[a].T
+    w_out[:, :, pl.ds(pl.multiple_of((1 - c) * 256, 256), 256)] = fsib[...]
+
+
+def finish(*refs):
+    given, results, held, (load, store) = refs[0:3], refs[3:6], refs[6:9], refs[9:11]
+    parts = []
+    for i in range(3):
+        rows = given[i].shape[-2] // 4
+        for k in range(4):
+            at = (slice(None),) * (len(given[i].shape) - 2) + (pl.ds(k * rows, rows),)
+            parts.append(
+                (
+                    pltpu.make_async_copy(given[i].at[at], held[i].at[at], load.at[i, k]),
+                    pltpu.make_async_copy(held[i].at[at], results[i].at[at], store.at[i, k]),
+                )
+            )
+    for first, _ in parts:
+        first.start()
+    for first, second in parts:
+        first.wait()
+        second.start()
+    for _, second in parts:
+        second.wait()
 
 
 VM = pl.BlockSpec(memory_space=pltpu.VMEM)
@@ -756,7 +779,7 @@
             pltpu.VMEM((8, 256, 512), BF),
             pltpu.VMEM((8, 512, 128), BF),
             pltpu.VMEM((4096, 512), F32),
-            pltpu.VMEM((4096, 512), BF),
+            pltpu.VMEM((4096, 256), BF),
             pltpu.VMEM((4096, 128), F32),
             DMA((2,)), DMA((8,)), DMA((8,)),
         ],
@@ -764,9 +787,9 @@
         name="attend",
     )(spans, kvx, kvt, xt, xs)
 
-    enc_t, qg, w_t = pl.pallas_call(
+    grads = pl.pallas_call(
         back,
-        out_shape=(shape((1024, 256), BF), shape((8, 128, 128), BF), shape((2, 512, 128), F32)),
+        out_shape=(shape((256, 1024), BF), shape((256, 512), BF), shape((2, 128, 512), F32)),
         in_specs=[ANY, ANY, ANY, ANY],
         out_specs=(VM, VM, VM),
         scratch_shapes=[
@@ -785,7 +808,7 @@
             pltpu.VMEM((2, 5, 2, 256, 256), BF),
             pltpu.VMEM((2, 4, 256, 256), F32),
             pltpu.VMEM((2, 256, 256), F32),
-            pltpu.VMEM((2, 256, 128), F32),
+            pltpu.VMEM((2, 128, 256), F32),
             pltpu.VMEM((2, 2, 256, 256), BF),
             pltpu.VMEM((2, 2, 256, 256), BF),
             pltpu.VMEM((2, 2, 2, 256, 256), BF),
@@ -804,11 +827,15 @@
     enc_grad, q_grad, w_grad = pl.pallas_call(
         finish,
         out_shape=(shape((256, 1024), BF), shape((256, 512), BF), shape((2, 128, 512), F32)),
-        in_specs=[VM] * 3,
-        out_specs=(VM, VM, VM),
+        in_specs=[ANY] * 3,
+        out_specs=(ANY, ANY, ANY),
+        scratch_shapes=[
+            pltpu.VMEM((256, 1024), BF), pltpu.VMEM((256, 512), BF), pltpu.VMEM((2, 128, 512), F32),
+            DMA((3, 4)), DMA((3, 4)),
+        ],
         compiler_params=params(),
         name="finish",
-    )(enc_t, qg, w_t)
+    )(*grads)
     return enc_grad[None], q_grad[None], w_grad
 
 

time: 130 us -> 128 us (0.985)
  Pallas kernels: 129 us -> 127 us
    pallas_call x1, Pallas kernels: 23.9 us -> 15 us  [body(): pl.pallas_call(attend, out_shape=(shape((8, 512, 128), BF), shape((8, 128...]
    pallas_call x1, Pallas kernels: 47.9 us -> 54.6 us  [body(): pl.pallas_call(back, out_shape=(shape((256, 1024), BF), shape((256, 512),...]
where the time goes in v4:
time: 128 us
  Pallas kernels  127 us (99%)
    pallas_call x1, Pallas kernels, body(): pl.pallas_call(front, out_shape=(shape((2, 4, 4, 256, 256), BF), shape((4...  55 us
    pallas_call x1, Pallas kernels, body(): pl.pallas_call(back, out_shape=(shape((256, 1024), BF), shape((256, 512),...  54.6 us
    pallas_call x1, Pallas kernels, body(): pl.pallas_call(attend, out_shape=(shape((8, 512, 128), BF), shape((8, 128...  15 us

profile of v4, /device:TPU:1, one launch (start us, length us, event | category | flops | bytes accessed | tf_op | source)
XLA Modules:
  0.0 127.7 jit_solution(5065761505784207970)
XLA Ops:
  0.6 55.0 %front.1 = (bf16[2,4,4,256,256]{4,3,2,1,0:T(8,128)(2,1)}, bf16[4096,256]{1,0:T(8,128)(2,1)}, bf16[128,4096]{1,0:T(8,128)(2,1)}, bf16[8,256,512]{2,1,0:T(8,128)(2...) custom-call(bf16[256,4096]{1,0:T(8,128)(2,1)} %bitcast.7, bf16[256,512]{1,0:T(8,128)(2,1)} %bitcast.9, ...), custom_call_target="tpu_custom_call" | custom-call | tf_op jit(solution)/shard_map/front/pallas_call | solution.py:737
  55.6 15.0 %attend.1 = (bf16[8,512,128]{2,1,0:T(8,128)(2,1)}, bf16[8,128,128]{2,1,0:T(8,128)(2,1)}) custom-call(s32[8,128]{1,0:T(8,128)} %get-tuple-element.17.spans, bf16[4096,256]{1,0:T(8,128)(2,1)} %get-tuple-element.18.kvx_in, bf16[128,4096]{1,0:T(8,128)(2,1)} %get-tuple-element.19.kvt_in, bf16[8,256,512]{2,1,0:T(8,128)(2,1)} %get-tuple-element.20.xt_in, ...), custom_call_target="tpu_custom_call" | custom-call | tf_op jit(solution)/shard_map/attend/pallas_call | solution.py:771
  70.7 54.6 %back.1 = (bf16[256,1024]{1,0:T(8,128)(2,1)}, bf16[256,512]{1,0:T(8,128)(2,1)}, f32[2,128,512]{2,1,0:T(8,128)}) custom-call(bf16[8,512,128]{2,1,0:T(8,128)(2,1)} %get-tuple-element.22.dkvp, bf16[8,128,128]{2,1,0:T(8,128)(2,1)} %get-tuple-element.23.dqp, bf16[256,4096]{1,0:T(8,128)(2,1)} %bitcast.8, bf16[2,4,4,256,256]{4,3,2,1,0:T(8,128)(2,1)} %get-tuple-element.24.w), custom_call_target="tpu_custom_call" | custom-call | tf_op jit(solution)/shard_map/back/pallas_call | solution.py:790
  125.3 2.2 %finish.1 = (bf16[256,1024]{1,0:T(8,128)(2,1)}, bf16[256,512]{1,0:T(8,128)(2,1)}, f32[2,128,512]{2,1,0:T(8,128)}) custom-call(bf16[256,1024]{1,0:T(8,128)(2,1)} %get-tuple-element.25.refs_0_, bf16[256,512]{1,0:T(8,128)(2,1)} %get-tuple-element.26.refs_1_, f32[2,128,512]{2,1,0:T(8,128)} %get-tuple-element.27.refs_2_), custom_call_target="tpu_custom_call" | custom-call | tf_op jit(solution)/shard_map/finish/pallas_call | solution.py:827

commit v5 on v4

--- a/solution.py
+++ b/solution.py
@@ -28,6 +28,10 @@
     return (x % 2) * 2 + x // 2
 
 
+def swap(v):
+    return (v % 2) * 2 + v // 2
+
+
 def mod4(v):
     return (v + 4) % 4
 
@@ -51,12 +55,12 @@
     pl.semaphore_wait(pltpu.get_barrier_semaphore(), len(peers))
 
 
-def plane_peers(x, z, c, y):
+def plane_peers(x, z, c, y, other_cores):
     peers = [dev(x, z, 1 - c, y), dev(mod4(x + 1), z, c, y), dev(mod4(x + 3), z, c, y)]
-    for dx in (0, 2):
+    for dx, core in [(0, c), (2, c)] + other_cores:
         for dz in range(4):
             if dx or dz:
-                peers += [dev(mod4(x + dx), mod4(z + dz), core, y) for core in range(2)]
+                peers.append(dev(mod4(x + dx), mod4(z + dz), core, y))
     return peers
 
 
@@ -71,40 +75,59 @@
 
 
 def front(
-    enc, q, do, w, dseg, eseg,
+    enc, q_in, do_in, w, dseg, eseg,
     wg_out, kvx_out, kvt_out, xt_out, xs_out, spans,
-    encv, wg, acc, kvs, kvb, qs, qb, kvx, kvt, xt, xs,
+    encv, wg, acc, kvs, kvb, q, do, qs, qb, kvx, kvt, xt, xs,
     loc, save, sib_s, sib_r, ws, wr, qsend, qrecv, ksend, krecv, fsend, frecv,
 ):
     x, xh, z, c, y = coords()
     me = row_group(x)
     t = xh * 4 + z
     sibling = dev(x, z, 1 - c, y)
-    peers = plane_peers(x, z, c, y)
+    peers = plane_peers(x, z, c, y, [(0, 1 - c), (2, 1 - c)])
+    q_in_copy = pltpu.make_async_copy(q_in, q, loc.at[5])
+    do_in_copy = pltpu.make_async_copy(do_in, do, loc.at[6])
+    q_in_copy.start()
+    do_in_copy.start()
     greet(peers)
 
     own = pl.multiple_of(c * 256, 256)
     other = pl.multiple_of((1 - c) * 256, 256)
     rows = pl.ds(pl.multiple_of(c * 128, 128), 128)
-    w_loc = pltpu.make_async_copy(w.at[:, :, pl.ds(own, 256)], wg.at[:, me, z, rows], loc.at[0])
-    w_loc.start()
+    w_loc = [
+        pltpu.make_async_copy(
+            w.at[:, :, pl.ds(own + 128 * part, 128)], wg.at[:, part, me, z, rows], loc.at[7 * part]
+        )
+        for part in range(2)
+    ]
+    for copy in w_loc:
+        copy.start()
     e_loc = pltpu.make_async_copy(enc, encv.at[c], loc.at[1])
     e_loc.start()
 
     ids = dseg[...].astype(F32)
     row = lax.broadcasted_iota(jnp.int32, (16, 128), 0)
     id_rows = jnp.where(row == 0, ids[0:1], jnp.where(row == 1, ids[1:2], 0.0)).astype(BF)
+    q_in_copy.wait()
+    do_in_copy.wait()
     for h in range(8):
         tile = pl.ds((h // 2) * 128, 128)
         odd = h % 2 == 1
         qs[h, 0:256, :] = halves(q[:, tile].astype(F32), do[:, tile].astype(F32), odd, not odd).astype(BF)
         qs[h, 256:272, :] = id_rows
-    q_loc = pltpu.make_async_copy(qs.at[t], qb.at[t], loc.at[2])
+    q_loc = pltpu.make_async_copy(qs.at[xh * 4 + swap(z)], qb.at[t], loc.at[2])
     q_loc.start()
     greeted(peers)
 
-    w_sib = remote(w.at[:, :, pl.ds(other, 256)], wg.at[:, me, z, rows], sib_s.at[0], sib_r.at[0], sibling)
-    w_sib.start()
+    w_sib = [
+        remote(
+            w.at[:, :, pl.ds(other + 128 * part, 128)], wg.at[:, part, me, z, rows],
+            sib_s.at[2 * part], sib_r.at[2 * part], sibling,
+        )
+        for part in range(2)
+    ]
+    for copy in w_sib:
+        copy.start()
     q_sent = []
     for dxh in (1, 0):
         for dz in (2, 1, 3, 0):
@@ -112,63 +135,93 @@
                 continue
             hx, hz = (xh + dxh) % 2, mod4(z + dz)
             copy = remote(
-                qs.at[hx * 4 + hz], qb.at[t], qsend.at[dxh, dz], qrecv.at[dxh, dz],
+                qs.at[hx * 4 + swap(hz)], qb.at[t], qsend.at[dxh, dz], qrecv.at[dxh, dz],
                 dev(mod4(x + 2 * dxh), hz, c, y),
             )
             copy.start()
             q_sent.append(copy)
     e_sib = remote(enc, encv.at[c], sib_s.at[1], sib_r.at[1], sibling)
     e_sib.start()
-    w_loc.wait()
-    w_sib.wait()
+    for copy in w_loc + w_sib:
+        copy.wait()
 
     def place(a, first, second):
         bx, bz = (first, second) if a == 0 else (second, first)
         return row_group(mod4(x - bx)), mod4(z - bz)
 
-    def block_of(a, first, second, half=None):
+    def block_of(part, a, first, second, half=None):
         group, bz = place(a, first, second)
-        block = wg.at[a, group, bz]
+        block = wg.at[a, part, group, bz]
         return block if half is None else block.at[pl.ds(half * 128, 128)]
 
     sent = []
 
-    def pass_on(a, first, second, ring, step, half=None):
-        block = block_of(a, first, second, half)
+    def pass_on(part, a, first, second, ring, step, half=None):
+        block = block_of(part, a, first, second, half)
         to_first, to_second = (first + step) % 4 if ring == 0 else first, (second + step) % 4 if ring else second
-        sem = (a, to_first, to_second, half or 0)
+        sem = (part, a, to_first, to_second, half or 0)
         along_x = (a == 0) == (ring == 0)
         target = dev(mod4(x + step), z, c, y) if along_x else dev(x, mod4(z + step), c, y)
         copy = remote(block, block, ws.at[sem], wr.at[sem], target)
         copy.start()
         sent.append(copy)
 
-    def take(a, first, second):
+    def take(part, a, first, second):
         if second == 2 or (first == 2 and second == 0):
             for half in range(2):
-                arrived(block_of(a, first, second, half), wr.at[a, first, second, half])
+                arrived(block_of(part, a, first, second, half), wr.at[part, a, first, second, half])
         else:
-            arrived(block_of(a, first, second), wr.at[a, first, second, 0])
-
-    def multiply(a, first, second, fresh=False):
-        group, bz = place(a, first, second)
+            arrived(block_of(part, a, first, second), wr.at[part, a, first, second, 0])
+
+    def multiply(part, dx, dz, fresh=False):
+        group, bz = place(0, dx, dz)
         columns = pl.ds(pl.multiple_of((group * 4 + bz) * 256, 256), 256)
+        both = jnp.concatenate([wg[0, part, group, bz], wg[1, part, group, bz]], axis=1)
         for half in range(2):
-            term = jnp.dot(encv[half, :, columns], wg[a, group, bz], preferred_element_type=F32)
+            term = jnp.dot(encv[half, :, columns], both, preferred_element_type=F32)
             if fresh:
-                acc[a, pl.ds(half * 256, 256), :] = term
+                acc[part, pl.ds(half * 256, 256), :] = term
             else:
-                acc[a, pl.ds(half * 256, 256), :] += term
-
-    def both_ways(a, first):
-        pass_on(a, first, 0, 1, 1)
-        pass_on(a, first, 0, 1, -1)
-
-    for step in (1, -1):
+                acc[part, pl.ds(half * 256, 256), :] += term
+
+    def both_ways(part, a, first):
+        pass_on(part, a, first, 0, 1, 1)
+        pass_on(part, a, first, 0, 1, -1)
+
+    def own_first(part):
+        for step in (1, -1):
+            for a in range(2):
+                pass_on(part, a, 0, 0, 0, step)
+
+    def own_second(part):
         for a in range(2):
-            pass_on(a, 0, 0, 0, step)
-    for a in range(2):
-        both_ways(a, 0)
+            both_ways(part, a, 0)
+
+    def near_first(part):
+        for a in range(2):
+            take(part, a, 1, 0)
+            pass_on(part, a, 1, 0, 0, 1, 0)
+            take(part, a, 3, 0)
+            pass_on(part, a, 3, 0, 0, -1, 1)
+        for a in range(2):
+            both_ways(part, a, 1)
+            both_ways(part, a, 3)
+
+    def near_second(part, first):
+        for a in range(2):
+            take(part, a, first, 1)
+            pass_on(part, a, first, 1, 1, 1, 0)
+            take(part, a, first, 3)
+            pass_on(part, a, first, 3, 1, -1, 1)
+
+    def far_first(part):
+        for a in range(2):
+            take(part, a, 2, 0)
+            both_ways(part, a, 2)
+
+    own_first(0)
+    own_second(0)
+    own_first(1)
 
     def one_hot(i, _):
         seg = eseg[pl.ds(i, 1), :].astype(F32)
@@ -179,28 +232,28 @@
 
     lax.fori_loop(0, 32, one_hot, 0)
 
-    for a in range(2):
-        take(a, 1, 0)
-        pass_on(a, 1, 0, 0, 1, 0)
-        take(a, 3, 0)
-        pass_on(a, 3, 0, 0, -1, 1)
-    for a in range(2):
-        both_ways(a, 1)
-        both_ways(a, 3)
-    for a in range(2):
-        take(a, 0, 1)
-        pass_on(a, 0, 1, 1, 1, 0)
-        take(a, 0, 3)
-        pass_on(a, 0, 3, 1, -1, 1)
-    for a in range(2):
-        take(a, 2, 0)
-        both_ways(a, 2)
+    near_first(0)
+    own_second(1)
+    near_second(0, 0)
+    near_first(1)
+    far_first(0)
+    near_second(1, 0)
+    far_first(1)
     e_loc.wait()
     e_sib.wait()
-    for a in range(2):
-        multiply(a, 0, 0, True)
-        for first, second in ((1, 0), (3, 0), (0, 1), (0, 3), (2, 0)):
-            multiply(a, first, second)
+
+    def multiply_near(part):
+        multiply(part, 0, 0, True)
+        for d in (1, 3):
+            multiply(part, d, 0)
+            multiply(part, 0, d)
+
+    def multiply_diagonal(part):
+        for dx in (1, 3):
+            for dz in (1, 3):
+                multiply(part, dx, dz)
+
+    multiply_near(0)
 
     q_loc.wait()
     for dxh in range(2):
@@ -236,60 +289,64 @@
         spans[pl.ds(b, 1), :] = jnp.where(lanes_of((1, 128)) == 0, begin, count).astype(jnp.int32)
         return 0
 
+    lax.fori_loop(0, 4, prepare, 0)
     for first in (1, 3, 2):
-        for a in range(2):
-            take(a, first, 1)
-            pass_on(a, first, 1, 1, 1, 0)
-            take(a, first, 3)
-            pass_on(a, first, 3, 1, -1, 1)
-            multiply(a, first, 1)
-            multiply(a, first, 3)
-        if first != 2:
-            lax.fori_loop(0 if first == 1 else 4, 4 if first == 1 else 8, prepare, 0)
+        near_second(0, first)
+    multiply_near(1)
+    for first in (1, 3, 2):
+        near_second(1, first)
+    multiply_diagonal(0)
+
+    ex = (c + 2 - xh) % 2
+    tx = c * 2 + x % 2
+    here = c == xh
+
+    def kv_copy(head, core):
+        rows_of = pl.ds(core * 256, 256)
+        return remote(
+            kvs.at[head, rows_of], kvb.at[t, rows_of], ksend.at[head, core], krecv.at[ex, z],
+            dev(tx, swap(head), core, y),
+        )
+
+    def kv_local(core):
+        rows_of = pl.ds(core * 256, 256)
+        return pltpu.make_async_copy(kvs.at[swap(z), rows_of], kvb.at[t, rows_of], loc.at[4])
+
+    def stays(head, core):
+        return jnp.logical_and(here, jnp.logical_and(z == swap(head), c == core))
+
+    def last_part(part):
+        for dx, dz in ((2, 0), (0, 2), (1, 2), (3, 2), (2, 1), (2, 3), (2, 2)):
+            if dz == 2:
+                take(part, 0, dx, dz)
+            if dx == 2:
+                take(part, 1, dz, dx)
+            multiply(part, dx, dz)
+        for i in range(2):
+            head = 2 * part + i
+            keys, values = acc[part, :, 0:128], acc[part, :, 128:256]
+            kvs[head] = halves(keys, values, i == 1, i == 0).astype(BF)
+            for core in range(2):
+                local = stays(head, core)
+
+                @pl.when(local)
+                def _():
+                    kv_local(core).start()
+
+                @pl.when(jnp.logical_not(local))
+                def _():
+                    kv_copy(head, core).start()
+
+    last_part(0)
+    multiply_diagonal(1)
+    last_part(1)
+    lax.fori_loop(4, 8, prepare, 0)
     saved = [
         pltpu.make_async_copy(xt, xt_out, save.at[8]),
         pltpu.make_async_copy(xs, xs_out, save.at[9]),
     ]
     for copy in saved:
         copy.start()
-    for first in (0, 1, 3, 2):
-        for a in range(2):
-            take(a, first, 2)
-            multiply(a, first, 2)
-
-    for j in range(4):
-        tile = pl.ds((j // 2) * 128, 128)
-        odd = j % 2 == 1
-        kvs[j] = halves(acc[0, :, tile], acc[1, :, tile], odd, not odd).astype(BF)
-
-    ex = (c + 2 - xh) % 2
-    tx = c * 2 + x % 2
-    here = c == xh
-
-    def kv_copy(dz, core):
-        hz = mod4(z + dz)
-        part = pl.ds(core * 256, 256)
-        return remote(
-            kvs.at[hz, part], kvb.at[t, part], ksend.at[dz, core], krecv.at[ex, dz], dev(tx, hz, core, y)
-        )
-
-    def kv_local(core):
-        part = pl.ds(core * 256, 256)
-        return pltpu.make_async_copy(kvs.at[z, part], kvb.at[t, part], loc.at[4])
-
-    k_sent = [kv_copy(dz, core) for dz in (2, 1, 3) for core in range(2)]
-    for copy in k_sent:
-        copy.start()
-    for core in range(2):
-        local = jnp.logical_and(here, c == core)
-
-        @pl.when(local)
-        def _():
-            kv_local(core).start()
-
-        @pl.when(jnp.logical_not(local))
-        def _():
-            kv_copy(0, core).start()
 
     w_save = pltpu.make_async_copy(wg, wg_out, loc.at[3])
     w_save.start()
@@ -316,9 +373,9 @@
 
             @pl.when(jnp.logical_not(here))
             def _():
-                arrived(kvb.at[src, mine], krecv.at[0, 0])
+                arrived(kvb.at[src, mine], krecv.at[0, z])
         else:
-            arrived(kvb.at[src, mine], krecv.at[e, dz])
+            arrived(kvb.at[src, mine], krecv.at[e, mod4(z - dz)])
         copy = remote(kvb.at[src, mine], kvb.at[src, mine], fsend.at[e, dz], frecv.at[e, dz], sibling)
         copy.start()
         f_sent.append(copy)
@@ -344,13 +401,14 @@
             use(*order[i - 1])
     use(*order[-1])
 
-    for copy in sent + q_sent + k_sent + f_sent:
+    for copy in sent + q_sent + f_sent:
         copy.wait_send()
-    for core in range(2):
-
-        @pl.when(jnp.logical_not(jnp.logical_and(here, c == core)))
-        def _():
-            kv_copy(0, core).wait_send()
+    for head in range(4):
+        for core in range(2):
+
+            @pl.when(jnp.logical_not(stays(head, core)))
+            def _():
+                kv_copy(head, core).wait_send()
 
     w_save.wait()
     for copy in saved:
@@ -358,7 +416,8 @@
 
 
 def attend(
-    spans, kvx_in, kvt_in, xt_in, xs_in, dkv_out, dq_out, kvx, kvt, xt, xs, tt, low_ps, dkv, sem, xt_sem, xs_sem
+    spans, kvx_in, kvt_in, xt_in, xs_in, dkv_res, dq_res,
+    kvx, kvt, xt, xs, tt, low_ps, dkv, dkv_out, dq_out, sem, xt_sem, xs_sem, dkv_sem, dq_sem,
 ):
     kvx_copy = pltpu.make_async_copy(kvx_in, kvx, sem.at[0])
     kvt_copy = pltpu.make_async_copy(kvt_in, kvt, sem.at[1])
@@ -444,21 +503,33 @@
 
         dq = sweep(grads, jnp.zeros((64, 256), F32))
         dq_out[b] = jnp.concatenate([dq[:, 0:128], dq[:, 128:256]], axis=0).T.astype(BF)
+        dq_copy(b).start()
         return 0
 
+    def dq_copy(b):
+        return pltpu.make_async_copy(dq_out.at[b], dq_res.at[b], dq_sem.at[b])
+
     lax.fori_loop(0, 8, one_block, 0)
-    dkv_out[...] = dkv[...].astype(BF).reshape(dkv_out.shape)
+    saved = []
+    for t in range(8):
+        dkv_out[t] = dkv[pl.ds(t * 512, 512), :].astype(BF)
+        saved.append(pltpu.make_async_copy(dkv_out.at[t], dkv_res.at[t], dkv_sem.at[t]))
+        saved[t].start()
+    for t in range(8):
+        saved[t].wait()
+        dq_copy(t).wait()
 
 
 def back(
     dkvp, dqp, enc, w,
-    enc_out, q_out, w_out,
-    encv, wv, po, pb, ps, rb, gt, gs, qg, cs, cr, ms, mr, keep, fin, fsib, ycs, ycr, yms, ymr,
+    enc_res, q_res, w_res,
+    enc_out, q_out, encv, wv, po, pb, ps, rb, gt, gs, qg, cs, cr, ms, mr, keep, fin, fsib, ycs, ycr, yms, ymr,
     loc, sib_s, sib_r, dsend, drecv, qsend, qrecv, csend, crecv, msend, mrecv, ysend, yrecv,
 ):
     x, xh, z, c, y = coords()
     sibling = dev(x, z, 1 - c, y)
-    peers = plane_peers(x, z, c, y) + [dev(x, z, c, mod4(y + 1)), dev(x, z, c, mod4(y + 3))]
+    peers = [dev(x, z, c, mod4(y + 1)), dev(x, z, c, mod4(y + 3))]
+    peers += plane_peers(x, z, c, y, [(2, 1 - c)])
     greet(peers)
     p_loc = pltpu.make_async_copy(dkvp.at[pl.ds(c * 4, 4)], po, loc.at[0])
     p_loc.start()
@@ -466,7 +537,7 @@
     e_loc.start()
     w_loc = pltpu.make_async_copy(w, wv.at[c], loc.at[2])
     w_loc.start()
-    q_loc = pltpu.make_async_copy(dqp.at[xh * 4 + z], qg.at[xh * 4 + z], loc.at[3])
+    q_loc = pltpu.make_async_copy(dqp.at[xh * 4 + z], qg.at[xh * 4 + swap(z)], loc.at[3])
     q_loc.start()
     greeted(peers)
 
@@ -505,7 +576,7 @@
             if dxh or dz:
                 tx, tz = (xh + dxh) % 2, mod4(z + dz)
                 copy = remote(
-                    dqp.at[tx * 4 + tz], qg.at[xh * 4 + z], qsend.at[dxh, dz], qrecv.at[dxh, dz],
+                    dqp.at[tx * 4 + tz], qg.at[xh * 4 + swap(z)], qsend.at[dxh, dz], qrecv.at[dxh, dz],
                     dev(tx * 2 + x % 2, tz, c, y),
                 )
                 copy.start()
@@ -525,7 +596,7 @@
         else:
             arrived(rb.at[j], drecv.at[dz])
         turned = rb[j].T
-        keys = pl.ds(pl.multiple_of(j * 64, 64), 64)
+        keys = pl.ds(pl.multiple_of(swap(j) * 64, 64), 64)
         gt[0, keys, :] = turned[0:64]
         gt[1, keys, :] = turned[64:128]
 
@@ -597,7 +668,8 @@
         total = None
         for half in range(2):
             for a in range(2):
-                term = jnp.dot(wv[half, a, group, r], gs[half, a], preferred_element_type=F32)
+                weights = jnp.concatenate([wv[half, a, 0, group, r], wv[half, a, 1, group, r]], axis=1)
+                term = jnp.dot(weights, gs[half, a], preferred_element_type=F32)
                 total = term if total is None else total + term
         return total
 
@@ -653,13 +725,15 @@
     for dxh in range(2):
         for dz in range(4):
             if dxh or dz:
-                src = ((xh + dxh) % 2) * 4 + mod4(z - dz)
+                src = ((xh + dxh) % 2) * 4 + swap(mod4(z - dz))
                 arrived(qg.at[src], qrecv.at[dxh, dz])
     for i in range(4):
         tile = pl.ds(i * 128, 128)
         even, odd = qg[2 * i].astype(F32), qg[2 * i + 1].astype(F32)
         q_out[0:128, tile] = halves(even, odd, False, True).astype(BF)
         q_out[128:256, tile] = halves(even, odd, True, False).astype(BF)
+    q_save = pltpu.make_async_copy(q_out, q_res, loc.at[6])
+    q_save.start()
 
     for a in range(2):
         for slot in (1, 3):
@@ -675,6 +749,8 @@
                 arrived(ymr.at[half, half], yrecv.at[4 + half])
             total = total + ymr[half, r // 2, r % 2].astype(F32)
         enc_out[:, pl.ds(r * 256, 256)] = total.T.astype(BF)
+    enc_save = pltpu.make_async_copy(enc_out, enc_res, loc.at[7])
+    enc_save.start()
 
     for a in range(2):
         fin[a] = collect(a, 4, collect(a, 0, keep[a, 0])).T
@@ -682,7 +758,15 @@
     theirs = pl.ds(pl.multiple_of((1 - c) * 128, 128), 128)
     f_sib = remote(fin.at[:, theirs], fsib, sib_s.at[4], sib_r.at[4], sibling)
     f_sib.start()
-    w_out[:, :, pl.ds(pl.multiple_of(c * 256, 256), 256)] = fin[:, mine]
+    w_own = pltpu.make_async_copy(
+        fin.at[:, mine], w_res.at[:, :, pl.ds(pl.multiple_of(c * 256, 256), 256)], loc.at[8]
+    )
+    w_own.start()
+    f_sib.wait()
+    w_other = pltpu.make_async_copy(
+        fsib, w_res.at[:, :, pl.ds(pl.multiple_of((1 - c) * 256, 256), 256)], loc.at[9]
+    )
+    w_other.start()
     for copy in q_sent + sent + [d_copy(dz) for dz in (1, 2, 3)]:
         copy.wait_send()
 
@@ -690,8 +774,8 @@
     def _():
         d_copy(0).wait_send()
 
-    f_sib.wait()
-    w_out[:, :, pl.ds(pl.multiple_of((1 - c) * 256, 256), 256)] = fsib[...]
+    for copy in (enc_save, q_save, w_own, w_other):
+        copy.wait()
 
 
 def finish(*refs):
@@ -737,29 +821,31 @@
     wg, kvx, kvt, xt, xs, spans = pl.pallas_call(
         front,
         out_shape=(
-            shape((2, 4, 4, 256, 256), BF),
+            shape((2, 2, 4, 4, 256, 128), BF),
             shape((4096, 256), BF),
             shape((128, 4096), BF),
             shape((8, 256, 512), BF),
             shape((8, 512, 128), BF),
             shape((8, 128), jnp.int32),
         ),
-        in_specs=[ANY, VM, VM, ANY, VM, VM],
+        in_specs=[ANY, ANY, ANY, ANY, VM, VM],
         out_specs=(ANY, ANY, ANY, ANY, ANY, VM),
         scratch_shapes=[
             pltpu.VMEM((2, 256, 4096), BF),
-            pltpu.VMEM((2, 4, 4, 256, 256), BF),
+            pltpu.VMEM((2, 2, 4, 4, 256, 128), BF),
             pltpu.VMEM((2, 512, 256), F32),
             pltpu.VMEM((4, 512, 128), BF),
             pltpu.VMEM((8, 512, 128), BF),
+            pltpu.VMEM((256, 512), BF),
+            pltpu.VMEM((256, 512), BF),
             pltpu.VMEM((8, 272, 128), BF),
             pltpu.VMEM((8, 272, 128), BF),
             pltpu.VMEM((4096, 256), BF),
             pltpu.VMEM((128, 4096), BF),
             pltpu.VMEM((8, 256, 512), BF),
             pltpu.VMEM((8, 512, 128), BF),
-            DMA((5,)), DMA((18,)), DMA((2,)), DMA((2,)),
-            DMA((2, 4, 4, 2)), DMA((2, 4, 4, 2)),
+            DMA((8,)), DMA((18,)), DMA((3,)), DMA((3,)),
+            DMA((2, 2, 4, 4, 2)), DMA((2, 2, 4, 4, 2)),
             DMA((2, 4)), DMA((2, 4)),
             DMA((4, 2)), DMA((2, 4)),
             DMA((2, 4)), DMA((2, 4)),
@@ -772,7 +858,7 @@
         attend,
         out_shape=(shape((8, 512, 128), BF), shape((8, 128, 128), BF)),
         in_specs=[pl.BlockSpec(memory_space=pltpu.SMEM), ANY, ANY, ANY, ANY],
-        out_specs=(VM, VM),
+        out_specs=(ANY, ANY),
         scratch_shapes=[
             pltpu.VMEM((4096, 256), BF),
             pltpu.VMEM((128, 4096), BF),
@@ -781,7 +867,9 @@
             pltpu.VMEM((4096, 512), F32),
             pltpu.VMEM((4096, 256), BF),
             pltpu.VMEM((4096, 128), F32),
-            DMA((2,)), DMA((8,)), DMA((8,)),
+            pltpu.VMEM((8, 512, 128), BF),
+            pltpu.VMEM((8, 128, 128), BF),
+            DMA((2,)), DMA((8,)), DMA((8,)), DMA((8,)), DMA((8,)),
         ],
         compiler_params=params(),
         name="attend",
@@ -791,10 +879,12 @@
         back,
         out_shape=(shape((256, 1024), BF), shape((256, 512), BF), shape((2, 128, 512), F32)),
         in_specs=[ANY, ANY, ANY, ANY],
-        out_specs=(VM, VM, VM),
+        out_specs=(ANY, ANY, ANY),
         scratch_shapes=[
+            pltpu.VMEM((256, 1024), BF),
+            pltpu.VMEM((256, 512), BF),
             pltpu.VMEM((2, 256, 4096), BF),
-            pltpu.VMEM((2, 2, 4, 4, 256, 256), BF),
+            pltpu.VMEM((2, 2, 2, 4, 4, 256, 128), BF),
             pltpu.VMEM((4, 512, 128), BF),
             pltpu.VMEM((4, 512, 128), BF),
             pltpu.VMEM((4, 512, 128), BF),
@@ -813,7 +903,7 @@
             pltpu.VMEM((2, 2, 256, 256), BF),
             pltpu.VMEM((2, 2, 2, 256, 256), BF),
             pltpu.VMEM((2, 2, 2, 256, 256), BF),
-            DMA((6,)), DMA((5,)), DMA((5,)),
+            DMA((10,)), DMA((5,)), DMA((5,)),
             DMA((4,)), DMA((4,)),
             DMA((2, 4)), DMA((2, 4)),
             DMA((2, 5, 2)), DMA((2, 5, 2)),

time: 128 us -> 123 us (0.961)
  Pallas kernels: 127 us -> 122 us
    pallas_call x1, Pallas kernels: 54.6 us -> 51 us  [body(): pl.pallas_call(back, out_shape=(shape((256, 1024), BF), shape((256, 512),...]
    pallas_call x1, Pallas kernels: 55 us -> 52.4 us  [body(): pl.pallas_call(front, out_shape=(shape((2, 2, 4, 4, 256, 128), BF), shape...]
    pallas_call x1, Pallas kernels: 15 us -> 16.4 us  [body(): pl.pallas_call(attend, out_shape=(shape((8, 512, 128), BF), shape((8, 128...]
where the time goes in v5:
time: 123 us
  Pallas kernels  122 us (99%)
    pallas_call x1, Pallas kernels, body(): pl.pallas_call(front, out_shape=(shape((2, 2, 4, 4, 256, 128), BF), shape...  52.4 us
    pallas_call x1, Pallas kernels, body(): pl.pallas_call(back, out_shape=(shape((256, 1024), BF), shape((256, 512),...  51 us
    pallas_call x1, Pallas kernels, body(): pl.pallas_call(attend, out_shape=(shape((8, 512, 128), BF), shape((8, 128...  16.4 us

profile of v5, /device:TPU:1, one launch (start us, length us, event | category | flops | bytes accessed | tf_op | source)
XLA Modules:
  0.0 122.8 jit_solution(17353283965311470727)
XLA Ops:
  0.6 52.4 %front.1 = (bf16[2,2,4,4,256,128]{5,4,3,2,1,0:T(8,128)(2,1)}, bf16[4096,256]{1,0:T(8,128)(2,1)}, bf16[128,4096]{1,0:T(8,128)(2,1)}, bf16[8,256,512]{2,1,0:T(8,12...) custom-call(bf16[256,4096]{1,0:T(8,128)(2,1)} %bitcast.7, bf16[256,512]{1,0:T(8,128)(2,1)} %bitcast.9, ...), custom_call_target="tpu_custom_call" | custom-call | tf_op jit(solution)/shard_map/front/pallas_call | solution.py:821
  53.0 16.4 %attend.1 = (bf16[8,512,128]{2,1,0:T(8,128)(2,1)}, bf16[8,128,128]{2,1,0:T(8,128)(2,1)}) custom-call(s32[8,128]{1,0:T(8,128)} %get-tuple-element.17.spans, bf16[4096,256]{1,0:T(8,128)(2,1)} %get-tuple-element.18.kvx_in, bf16[128,4096]{1,0:T(8,128)(2,1)} %get-tuple-element.19.kvt_in, bf16[8,256,512]{2,1,0:T(8,128)(2,1)} %get-tuple-element.20.xt_in, ...), custom_call_target="tpu_custom_call" | custom-call | tf_op jit(solution)/shard_map/attend/pallas_call | solution.py:857
  69.4 51.0 %back.1 = (bf16[256,1024]{1,0:T(8,128)(2,1)}, bf16[256,512]{1,0:T(8,128)(2,1)}, f32[2,128,512]{2,1,0:T(8,128)}) custom-call(bf16[8,512,128]{2,1,0:T(8,128)(2,1)} %get-tuple-element.22.dkvp, bf16[8,128,128]{2,1,0:T(8,128)(2,1)} %get-tuple-element.23.dqp, bf16[256,4096]{1,0:T(8,128)(2,1)} %bitcast.8, bf16[2,2,4,4,256,128]{5,4,3,2,1,0:T(8,128)(2,1)} %get-tuple-element.24.w), custom_call_target="tpu_custom_call" | custom-call | tf_op jit(solution)/shard_map/back/pallas_call | solution.py:878
  120.4 2.2 %finish.1 = (bf16[256,1024]{1,0:T(8,128)(2,1)}, bf16[256,512]{1,0:T(8,128)(2,1)}, f32[2,128,512]{2,1,0:T(8,128)}) custom-call(bf16[256,1024]{1,0:T(8,128)(2,1)} %get-tuple-element.25.refs_0_, bf16[256,512]{1,0:T(8,128)(2,1)} %get-tuple-element.26.refs_1_, f32[2,128,512]{2,1,0:T(8,128)} %get-tuple-element.27.refs_2_), custom_call_target="tpu_custom_call" | custom-call | tf_op jit(solution)/shard_map/finish/pallas_call | solution.py:917

commit v6 on v5

--- a/solution.py
+++ b/solution.py
@@ -75,9 +75,9 @@
 
 
 def front(
-    enc, q_in, do_in, w, dseg, eseg,
-    wg_out, kvx_out, kvt_out, xt_out, xs_out, spans,
-    encv, wg, acc, kvs, kvb, q, do, qs, qb, kvx, kvt, xt, xs,
+    enc, q_in, do_in, w, dseg_in, eseg_in,
+    wg_out, kvx_out, kvt_out, xt_out, xs_out, spans_out,
+    encv, wg, acc, kvs, kvb, q, do, dseg, eseg, qs, qb, kvx, kvt, xt, xs, spans,
     loc, save, sib_s, sib_r, ws, wr, qsend, qrecv, ksend, krecv, fsend, frecv,
 ):
     x, xh, z, c, y = coords()
@@ -87,8 +87,10 @@
     peers = plane_peers(x, z, c, y, [(0, 1 - c), (2, 1 - c)])
     q_in_copy = pltpu.make_async_copy(q_in, q, loc.at[5])
     do_in_copy = pltpu.make_async_copy(do_in, do, loc.at[6])
-    q_in_copy.start()
-    do_in_copy.start()
+    dseg_copy = pltpu.make_async_copy(dseg_in, dseg, loc.at[8])
+    eseg_copy = pltpu.make_async_copy(eseg_in, eseg, loc.at[9])
+    for copy in (q_in_copy, do_in_copy, dseg_copy, eseg_copy):
+        copy.start()
     greet(peers)
 
     own = pl.multiple_of(c * 256, 256)
@@ -105,6 +107,8 @@
     e_loc = pltpu.make_async_copy(enc, encv.at[c], loc.at[1])
     e_loc.start()
 
+    dseg_copy.wait()
+    eseg_copy.wait()
     ids = dseg[...].astype(F32)
     row = lax.broadcasted_iota(jnp.int32, (16, 128), 0)
     id_rows = jnp.where(row == 0, ids[0:1], jnp.where(row == 1, ids[1:2], 0.0)).astype(BF)
@@ -344,6 +348,7 @@
     saved = [
         pltpu.make_async_copy(xt, xt_out, save.at[8]),
         pltpu.make_async_copy(xs, xs_out, save.at[9]),
+        pltpu.make_async_copy(spans, spans_out, save.at[18]),
     ]
     for copy in saved:
         copy.start()
@@ -416,8 +421,8 @@
 
 
 def attend(
-    spans, kvx_in, kvt_in, xt_in, xs_in, dkv_res, dq_res,
-    kvx, kvt, xt, xs, tt, low_ps, dkv, dkv_out, dq_out, sem, xt_sem, xs_sem, dkv_sem, dq_sem,
+    spans_in, kvx_in, kvt_in, xt_in, xs_in, dkv_res, dq_res,
+    spans, kvx, kvt, xt, xs, tt, low_ps, dkv, dkv_out, dq_out, sem, xt_sem, xs_sem, dkv_sem, dq_sem,
 ):
     kvx_copy = pltpu.make_async_copy(kvx_in, kvx, sem.at[0])
     kvt_copy = pltpu.make_async_copy(kvt_in, kvt, sem.at[1])
@@ -428,6 +433,8 @@
     def xs_copy(b):
         return pltpu.make_async_copy(xs_in.at[b], xs.at[b], xs_sem.at[b])
 
+    spans_copy = pltpu.make_async_copy(spans_in, spans, sem.at[2])
+    spans_copy.start()
     xt_copy(0).start()
     kvx_copy.start()
     xs_copy(0).start()
@@ -436,6 +443,7 @@
         xt_copy(b).start()
         xs_copy(b).start()
     dkv[...] = jnp.zeros_like(dkv)
+    spans_copy.wait()
     kvx_copy.wait()
 
     def one_block(b, _):
@@ -542,8 +550,11 @@
     greeted(peers)
 
     here = c == xh
-    p_sib = remote(dkvp.at[pl.ds((1 - c) * 4, 4)], pb, sib_s.at[0], sib_r.at[0], sibling)
-    p_sib.start()
+    p_sib = []
+    for i, dz in enumerate((2, 1, 3, 0)):
+        tz = mod4(z + dz)
+        p_sib.append(remote(dkvp.at[(1 - c) * 4 + tz], pb.at[tz], sib_s.at[5 + i], sib_r.at[5 + i], sibling))
+        p_sib[i].start()
     e_sib = remote(enc, encv.at[c], sib_s.at[1], sib_r.at[1], sibling)
     e_sib.start()
     w_sib = remote(w, wv.at[c], sib_s.at[2], sib_r.at[2], sibling)
@@ -554,9 +565,9 @@
         return remote(ps.at[tz], rb.at[z], dsend.at[dz], drecv.at[dz], dev(c * 2 + x % 2, tz, xh, y))
 
     p_loc.wait()
-    p_sib.wait()
-    for dz in (2, 1, 3, 0):
+    for i, dz in enumerate((2, 1, 3, 0)):
         tz = mod4(z + dz)
+        p_sib[i].wait()
         ps[tz] = (po[tz].astype(F32) + pb[tz].astype(F32)).astype(BF)
         if dz:
             d_copy(dz).start()
@@ -828,8 +839,8 @@
             shape((8, 512, 128), BF),
             shape((8, 128), jnp.int32),
         ),
-        in_specs=[ANY, ANY, ANY, ANY, VM, VM],
-        out_specs=(ANY, ANY, ANY, ANY, ANY, VM),
+        in_specs=[ANY] * 6,
+        out_specs=(ANY,) * 6,
         scratch_shapes=[
             pltpu.VMEM((2, 256, 4096), BF),
             pltpu.VMEM((2, 2, 4, 4, 256, 128), BF),
@@ -838,13 +849,16 @@
             pltpu.VMEM((8, 512, 128), BF),
             pltpu.VMEM((256, 512), BF),
             pltpu.VMEM((256, 512), BF),
+            pltpu.VMEM((2, 128), jnp.int32),
+            pltpu.VMEM((32, 128), jnp.int32),
             pltpu.VMEM((8, 272, 128), BF),
             pltpu.VMEM((8, 272, 128), BF),
             pltpu.VMEM((4096, 256), BF),
             pltpu.VMEM((128, 4096), BF),
             pltpu.VMEM((8, 256, 512), BF),
             pltpu.VMEM((8, 512, 128), BF),
-            DMA((8,)), DMA((18,)), DMA((3,)), DMA((3,)),
+            pltpu.VMEM((8, 128), jnp.int32),
+            DMA((10,)), DMA((19,)), DMA((3,)), DMA((3,)),
             DMA((2, 2, 4, 4, 2)), DMA((2, 2, 4, 4, 2)),
             DMA((2, 4)), DMA((2, 4)),
             DMA((4, 2)), DMA((2, 4)),
@@ -857,9 +871,10 @@
     dkvp, dqp = pl.pallas_call(
         attend,
         out_shape=(shape((8, 512, 128), BF), shape((8, 128, 128), BF)),
-        in_specs=[pl.BlockSpec(memory_space=pltpu.SMEM), ANY, ANY, ANY, ANY],
+        in_specs=[ANY] * 5,
         out_specs=(ANY, ANY),
         scratch_shapes=[
+            pltpu.SMEM((8, 128), jnp.int32),
             pltpu.VMEM((4096, 256), BF),
             pltpu.VMEM((128, 4096), BF),
             pltpu.VMEM((8, 256, 512), BF),
@@ -869,7 +884,7 @@
             pltpu.VMEM((4096, 128), F32),
             pltpu.VMEM((8, 512, 128), BF),
             pltpu.VMEM((8, 128, 128), BF),
-            DMA((2,)), DMA((8,)), DMA((8,)), DMA((8,)), DMA((8,)),
+            DMA((3,)), DMA((8,)), DMA((8,)), DMA((8,)), DMA((8,)),
         ],
         compiler_params=params(),
         name="attend",
@@ -903,7 +918,7 @@
             pltpu.VMEM((2, 2, 256, 256), BF),
             pltpu.VMEM((2, 2, 2, 256, 256), BF),
             pltpu.VMEM((2, 2, 2, 256, 256), BF),
-            DMA((10,)), DMA((5,)), DMA((5,)),
+            DMA((10,)), DMA((9,)), DMA((9,)),
             DMA((4,)), DMA((4,)),
             DMA((2, 4)), DMA((2, 4)),
             DMA((2, 5, 2)), DMA((2, 5, 2)),

time: 123 us -> 120 us (0.976)
  Pallas kernels: 122 us -> 119 us
    pallas_call x1, Pallas kernels: 16.4 us -> 12.4 us  [body(): pl.pallas_call(attend, out_shape=(shape((8, 512, 128), BF), shape((8, 128...]
    pallas_call x1, Pallas kernels: 51 us -> 53.4 us  [body(): pl.pallas_call(back, out_shape=(shape((256, 1024), BF), shape((256, 512),...]
where the time goes in v6:
time: 120 us
  Pallas kernels  119 us (99%)
    pallas_call x1, Pallas kernels, body(): pl.pallas_call(back, out_shape=(shape((256, 1024), BF), shape((256, 512),...  53.4 us
    pallas_call x1, Pallas kernels, body(): pl.pallas_call(front, out_shape=(shape((2, 2, 4, 4, 256, 128), BF), shape...  51.2 us
    pallas_call x1, Pallas kernels, body(): pl.pallas_call(attend, out_shape=(shape((8, 512, 128), BF), shape((8, 128...  12.4 us

profile of v6, /device:TPU:1, one launch (start us, length us, event | category | flops | bytes accessed | tf_op | source)
XLA Modules:
  0.0 120.1 jit_solution(3771485353800614952)
XLA Ops:
  0.6 51.2 %front.1 = (bf16[2,2,4,4,256,128]{5,4,3,2,1,0:T(8,128)(2,1)}, bf16[4096,256]{1,0:T(8,128)(2,1)}, bf16[128,4096]{1,0:T(8,128)(2,1)}, bf16[8,256,512]{2,1,0:T(8,12...) custom-call(bf16[256,4096]{1,0:T(8,128)(2,1)} %bitcast.7, bf16[256,512]{1,0:T(8,128)(2,1)} %bitcast.9, ...), custom_call_target="tpu_custom_call" | custom-call | tf_op jit(solution)/shard_map/front/pallas_call | solution.py:832
  51.9 12.4 %attend.1 = (bf16[8,512,128]{2,1,0:T(8,128)(2,1)}, bf16[8,128,128]{2,1,0:T(8,128)(2,1)}) custom-call(s32[8,128]{1,0:T(8,128)} %get-tuple-element.17.spans_in, bf16[4096,256]{1,0:T(8,128)(2,1)} %get-tuple-element.18.kvx_in, bf16[128,4096]{1,0:T(8,128)(2,1)} %get-tuple-element.19.kvt_in, bf16[8,256,512]{2,1,0:T(8,128)(2,1)} %get-tuple-element.20.xt_in, ...), custom_call_target="tpu_custom_call" | custom-call | tf_op jit(solution)/shard_map/attend/pallas_call | solution.py:871
  64.2 53.4 %back.1 = (bf16[256,1024]{1,0:T(8,128)(2,1)}, bf16[256,512]{1,0:T(8,128)(2,1)}, f32[2,128,512]{2,1,0:T(8,128)}) custom-call(bf16[8,512,128]{2,1,0:T(8,128)(2,1)} %get-tuple-element.22.dkvp, bf16[8,128,128]{2,1,0:T(8,128)(2,1)} %get-tuple-element.23.dqp, bf16[256,4096]{1,0:T(8,128)(2,1)} %bitcast.8, bf16[2,2,4,4,256,128]{5,4,3,2,1,0:T(8,128)(2,1)} %get-tuple-element.24.w), custom_call_target="tpu_custom_call" | custom-call | tf_op jit(solution)/shard_map/back/pallas_call | solution.py:893
  117.7 2.2 %finish.1 = (bf16[256,1024]{1,0:T(8,128)(2,1)}, bf16[256,512]{1,0:T(8,128)(2,1)}, f32[2,128,512]{2,1,0:T(8,128)}) custom-call(bf16[256,1024]{1,0:T(8,128)(2,1)} %get-tuple-element.25.refs_0_, bf16[256,512]{1,0:T(8,128)(2,1)} %get-tuple-element.26.refs_1_, f32[2,128,512]{2,1,0:T(8,128)} %get-tuple-element.27.refs_2_), custom_call_target="tpu_custom_call" | custom-call | tf_op jit(solution)/shard_map/finish/pallas_call | solution.py:932

commit v7 on v6

--- a/solution.py
+++ b/solution.py
@@ -399,6 +399,8 @@
             copy.start()
             saved.append(copy)
 
+    for copy in sent + q_sent:
+        copy.wait_send()
     order = [(e, dz) for dz in (0, 1, 3, 2) for e in (0, 1)]
     for i, at in enumerate(order):
         hand_over(*at)
@@ -406,7 +408,7 @@
             use(*order[i - 1])
     use(*order[-1])
 
-    for copy in sent + q_sent + f_sent:
+    for copy in f_sent:
         copy.wait_send()
     for head in range(4):
         for core in range(2):
@@ -541,7 +543,8 @@
     greet(peers)
     p_loc = pltpu.make_async_copy(dkvp.at[pl.ds(c * 4, 4)], po, loc.at[0])
     p_loc.start()
-    e_loc = pltpu.make_async_copy(enc, encv.at[c], loc.at[1])
+    tokens = pl.ds(pl.multiple_of(c * 256, 256), 256)
+    e_loc = pltpu.make_async_copy(enc, encv.at[tokens], loc.at[1])
     e_loc.start()
     w_loc = pltpu.make_async_copy(w, wv.at[c], loc.at[2])
     w_loc.start()
@@ -555,32 +558,6 @@
         tz = mod4(z + dz)
         p_sib.append(remote(dkvp.at[(1 - c) * 4 + tz], pb.at[tz], sib_s.at[5 + i], sib_r.at[5 + i], sibling))
         p_sib[i].start()
-    e_sib = remote(enc, encv.at[c], sib_s.at[1], sib_r.at[1], sibling)
-    e_sib.start()
-    w_sib = remote(w, wv.at[c], sib_s.at[2], sib_r.at[2], sibling)
-    w_sib.start()
-
-    def d_copy(dz):
-        tz = mod4(z + dz)
-        return remote(ps.at[tz], rb.at[z], dsend.at[dz], drecv.at[dz], dev(c * 2 + x % 2, tz, xh, y))
-
-    p_loc.wait()
-    for i, dz in enumerate((2, 1, 3, 0)):
-        tz = mod4(z + dz)
-        p_sib[i].wait()
-        ps[tz] = (po[tz].astype(F32) + pb[tz].astype(F32)).astype(BF)
-        if dz:
-            d_copy(dz).start()
-    d_loc = pltpu.make_async_copy(ps.at[z], rb.at[z], loc.at[4])
-
-    @pl.when(here)
-    def _():
-        d_loc.start()
-
-    @pl.when(jnp.logical_not(here))
-    def _():
-        d_copy(0).start()
-
     q_sent = []
     for dxh in (1, 0):
         for dz in (2, 1, 3, 0):
@@ -592,6 +569,31 @@
                 )
                 copy.start()
                 q_sent.append(copy)
+    e_sib = remote(enc, encv.at[tokens], sib_s.at[1], sib_r.at[1], sibling)
+    e_sib.start()
+    w_sib = remote(w, wv.at[c], sib_s.at[2], sib_r.at[2], sibling)
+    w_sib.start()
+
+    def d_copy(dz):
+        tz = mod4(z + dz)
+        return remote(ps.at[tz], rb.at[z], dsend.at[dz], drecv.at[dz], dev(c * 2 + x % 2, tz, xh, y))
+
+    p_loc.wait()
+    for i, dz in enumerate((2, 1, 3, 0)):
+        tz = mod4(z + dz)
+        p_sib[i].wait()
+        ps[tz] = (po[tz].astype(F32) + pb[tz].astype(F32)).astype(BF)
+        if dz:
+            d_copy(dz).start()
+    d_loc = pltpu.make_async_copy(ps.at[z], rb.at[z], loc.at[4])
+
+    @pl.when(here)
+    def _():
+        d_loc.start()
+
+    @pl.when(jnp.logical_not(here))
+    def _():
+        d_copy(0).start()
 
     for dz in (0, 1, 3, 2):
         j = mod4(z - dz)
@@ -623,9 +625,7 @@
     def product(a, first, second):
         bx, bz = (second, first) if a == 0 else (first, second)
         columns = pl.ds(pl.multiple_of((row_group(mod4(x + bx)) * 4 + mod4(z + bz)) * 256, 256), 256)
-        return jnp.dot(gt[a, :, 0:256], encv[0, :, columns], preferred_element_type=F32) + jnp.dot(
-            gt[a, :, 256:512], encv[1, :, columns], preferred_element_type=F32
-        )
+        return jnp.dot(gt[a], encv[:, columns], preferred_element_type=F32)
 
     sent = []
 
@@ -676,13 +676,10 @@
 
     def enc_rows(dy, r):
         group = mod4(y + dy)
-        total = None
-        for half in range(2):
-            for a in range(2):
-                weights = jnp.concatenate([wv[half, a, 0, group, r], wv[half, a, 1, group, r]], axis=1)
-                term = jnp.dot(weights, gs[half, a], preferred_element_type=F32)
-                total = term if total is None else total + term
-        return total
+        weights = [wv[half, a, part, group, r] for half in range(2) for a in range(2) for part in range(2)]
+        return jnp.dot(
+            jnp.concatenate(weights, axis=1), gs[...].reshape(1024, 256), preferred_element_type=F32
+        )
 
     def y_send(src, dst, i, step):
         copy = remote(src, dst, ysend.at[i], yrecv.at[i], dev(x, z, c, mod4(y + step)))
@@ -749,6 +746,7 @@
     for a in range(2):
         for slot in (1, 3):
             keep[a, slot] = collect(a, slot, keep[a, slot])
+    earlier = list(sent)
     for a in range(2):
         send_near(a, 4, 1, [lambda a=a: keep[a, 1], lambda a=a: keep[a, 3]])
 
@@ -762,6 +760,13 @@
         enc_out[:, pl.ds(r * 256, 256)] = total.T.astype(BF)
     enc_save = pltpu.make_async_copy(enc_out, enc_res, loc.at[7])
     enc_save.start()
+
+    for copy in q_sent + earlier + [d_copy(dz) for dz in (1, 2, 3)]:
+        copy.wait_send()
+
+    @pl.when(jnp.logical_not(here))
+    def _():
+        d_copy(0).wait_send()
 
     for a in range(2):
         fin[a] = collect(a, 4, collect(a, 0, keep[a, 0])).T
@@ -778,13 +783,8 @@
         fsib, w_res.at[:, :, pl.ds(pl.multiple_of((1 - c) * 256, 256), 256)], loc.at[9]
     )
     w_other.start()
-    for copy in q_sent + sent + [d_copy(dz) for dz in (1, 2, 3)]:
+    for copy in sent[len(earlier) :]:
         copy.wait_send()
-
-    @pl.when(jnp.logical_not(here))
-    def _():
-        d_copy(0).wait_send()
-
     for copy in (enc_save, q_save, w_own, w_other):
         copy.wait()
 
@@ -898,7 +898,7 @@
         scratch_shapes=[
             pltpu.VMEM((256, 1024), BF),
             pltpu.VMEM((256, 512), BF),
-            pltpu.VMEM((2, 256, 4096), BF),
+            pltpu.VMEM((512, 4096), BF),
             pltpu.VMEM((2, 2, 2, 4, 4, 256, 128), BF),
             pltpu.VMEM((4, 512, 128), BF),
             pltpu.VMEM((4, 512, 128), BF),

time: 120 us -> 118 us (0.983)
  Pallas kernels: 119 us -> 117 us
    pallas_call x1, Pallas kernels: 53.4 us -> 47.6 us  [body(): pl.pallas_call(back, out_shape=(shape((256, 1024), BF), shape((256, 512),...]
    pallas_call x1, Pallas kernels: 12.4 us -> 15.9 us  [body(): pl.pallas_call(attend, out_shape=(shape((8, 512, 128), BF), shape((8, 128...]
where the time goes in v7:
time: 118 us
  Pallas kernels  117 us (99%)
    pallas_call x1, Pallas kernels, body(): pl.pallas_call(front, out_shape=(shape((2, 2, 4, 4, 256, 128), BF), shape...  51.2 us
    pallas_call x1, Pallas kernels, body(): pl.pallas_call(back, out_shape=(shape((256, 1024), BF), shape((256, 512),...  47.6 us
    pallas_call x1, Pallas kernels, body(): pl.pallas_call(attend, out_shape=(shape((8, 512, 128), BF), shape((8, 128...  15.9 us

profile of v7, /device:TPU:1, one launch (start us, length us, event | category | flops | bytes accessed | tf_op | source)
XLA Modules:
  0.0 117.8 jit_solution(12412056676181324539)
XLA Ops:
  0.6 51.2 %front.1 = (bf16[2,2,4,4,256,128]{5,4,3,2,1,0:T(8,128)(2,1)}, bf16[4096,256]{1,0:T(8,128)(2,1)}, bf16[128,4096]{1,0:T(8,128)(2,1)}, bf16[8,256,512]{2,1,0:T(8,12...) custom-call(bf16[256,4096]{1,0:T(8,128)(2,1)} %bitcast.7, bf16[256,512]{1,0:T(8,128)(2,1)} %bitcast.9, ...), custom_call_target="tpu_custom_call" | custom-call | tf_op jit(solution)/shard_map/front/pallas_call | solution.py:832
  51.9 15.9 %attend.1 = (bf16[8,512,128]{2,1,0:T(8,128)(2,1)}, bf16[8,128,128]{2,1,0:T(8,128)(2,1)}) custom-call(s32[8,128]{1,0:T(8,128)} %get-tuple-element.17.spans_in, bf16[4096,256]{1,0:T(8,128)(2,1)} %get-tuple-element.18.kvx_in, bf16[128,4096]{1,0:T(8,128)(2,1)} %get-tuple-element.19.kvt_in, bf16[8,256,512]{2,1,0:T(8,128)(2,1)} %get-tuple-element.20.xt_in, ...), custom_call_target="tpu_custom_call" | custom-call | tf_op jit(solution)/shard_map/attend/pallas_call | solution.py:871
  67.8 47.6 %back.1 = (bf16[256,1024]{1,0:T(8,128)(2,1)}, bf16[256,512]{1,0:T(8,128)(2,1)}, f32[2,128,512]{2,1,0:T(8,128)}) custom-call(bf16[8,512,128]{2,1,0:T(8,128)(2,1)} %get-tuple-element.22.dkvp, bf16[8,128,128]{2,1,0:T(8,128)(2,1)} %get-tuple-element.23.dqp, bf16[256,4096]{1,0:T(8,128)(2,1)} %bitcast.8, bf16[2,2,4,4,256,128]{5,4,3,2,1,0:T(8,128)(2,1)} %get-tuple-element.24.w), custom_call_target="tpu_custom_call" | custom-call | tf_op jit(solution)/shard_map/back/pallas_call | solution.py:893
  115.4 2.2 %finish.1 = (bf16[256,1024]{1,0:T(8,128)(2,1)}, bf16[256,512]{1,0:T(8,128)(2,1)}, f32[2,128,512]{2,1,0:T(8,128)}) custom-call(bf16[256,1024]{1,0:T(8,128)(2,1)} %get-tuple-element.25.refs_0_, bf16[256,512]{1,0:T(8,128)(2,1)} %get-tuple-element.26.refs_1_, f32[2,128,512]{2,1,0:T(8,128)} %get-tuple-element.27.refs_2_), custom_call_target="tpu_custom_call" | custom-call | tf_op jit(solution)/shard_map/finish/pallas_call | solution.py:932
